TPU v7x, 128 devices: a whole 4x4x4 slice. The times are simulated.
128 devices in a mesh: gx: 8 (over y, core), gy: 16 (over z, x).
Axes of the slice: x: 4, y: 4, z: 4, core: 2. Of those that a mesh axis runs over, the one named last changes fastest.
Arguments:
- velocity: float32 [2, 512, 512, 128], P(None, 'gx', 'gy'), may hold values from -6 to 6
- metric: float32 [512, 512, 128], P('gx', 'gy'), may hold values from 0.7 to 1.4
- weights: float32 [262144, 128], P(('gx', 'gy')), may hold values from -0.5 to 0.5
- reynolds: float32 [262144], P(('gx', 'gy')), may hold values from 10 to 300
- face_tile: int32 [262144, 1], P(('gx', 'gy')), may hold values from 0 to 15; in each aligned block of 2048 rows (0 to 2047, 2048 to 4095, ...) at most 256 rows name the same one
- face_cell: int32 [262144], P(('gx', 'gy')), may hold values from 0 to 2047
- profile: float32 [128], replicated, may hold values from 2 to 20
Outputs:
- velocity_out: float32 [2, 512, 512, 128], P(None, 'gx', 'gy')
- stress: float32 [2, 262144], P(None, ('gx', 'gy'))
Inputs may be any that keep to these rules, and one draw needn't show every extreme that they name: `face_tile`: among the 2048 faces of one device, at most 256 name the same tile, and in every draw some device has a tile named by exactly 256 of its faces.
All inputs are finite; a program needn't handle non-finite values.
Results may differ from a plain program's by a relative error of at most 0.0001.
Values sent between devices are 32-bit elements; how exact they have to be, the bound alone decides.
A program may use at most 128 MiB of HBM per device.

v0:
```python
import jax
import jax.numpy as jnp
from jax import lax
from jax.experimental import pallas as pl
from jax.experimental.pallas import tpu as pltpu
from jax.sharding import PartitionSpec as P

WALL_ITERS = 3
CAP = 256
CX = 64
CY = 32
NZ = 128
FACES = 2048
SIDE = 4
GROUPS = SIDE * SIDE
SLOTS = GROUPS * CAP
CELLS = CX * CY
SPAN = (CX + 2) * CY
HALF = CAP // NZ

karman = 0.41
time_step = 0.2
viscosity = 0.5

MESH = pl.DeviceIdType.MESH
f32 = jnp.float32
bf16 = jnp.bfloat16
i32 = jnp.int32

NT = (((1,), (1,)), ((), ()))


def iota(shape, dim):
    return lax.broadcasted_iota(i32, shape, dim)


def mm(a, b):
    return jnp.dot(a, b, preferred_element_type=f32)


def mm_nt(a, b):
    return lax.dot_general(a, b, NT, preferred_element_type=f32)


def thirds(value):
    first = value.astype(bf16)
    rest = value - first.astype(f32)
    second = rest.astype(bf16)
    third = (rest - second.astype(f32)).astype(bf16)
    return first, second, third


def row_sums(product, ones, diagonal):
    first, second, third = thirds(product)
    total = mm(jnp.concatenate([first, second], axis=1), ones) + mm(third, ones[:NZ])
    rows = []
    for half in range(HALF):
        part = total[half * NZ : (half + 1) * NZ]
        rows.append(jnp.sum(jnp.where(diagonal, part, 0.0), axis=0, keepdims=True))
    return rows


def wall_stress(m0, m1, reynolds):
    speed = jnp.sqrt(m0 * m0 + m1 * m1 + 1.0)
    friction = 0.05 * speed
    for sweep in range(WALL_ITERS):
        friction = karman * speed / jnp.log(9.0 + reynolds * friction)
    factor = friction * friction / speed
    return factor * m0, factor * m1


def kernel(
    vel, met, wgt, rey_ref, tile_ref, cell_ref, prof_ref,
    out, stress_out,
    v0, v1, jac, win, wsend, wrecv, msend, mrecv, mine, lo_face, hi_face, a_face, b_face,
    meta_cell, meta_rey, cell_v, cell_s, inv_v, inv_s, cols, picked, dots, b_slot, a_slot, loads,
    hx, hy, hx2, hy2, ex, ey, ex2, ey2, vout, rsend, rrecv,
    in_sem, smem_sem, ms_sem, mr_sem, ws_sem, wr_sem, hs_sem, hr_sem, rs_sem, rr_sem, out_sem,
):
    gx = lax.axis_index("gx")
    gy = lax.axis_index("gy")
    mz = gy // SIDE
    mx = gy % SIDE

    def peer(step):
        return ((mz + step // SIDE) % SIDE) * SIDE + (mx + step % SIDE) % SIDE

    n_gx = lax.axis_size("gx")
    east = (lax.rem(gx + 1, n_gx), gy)
    west = (lax.rem(gx + n_gx - 1, n_gx), gy)
    north = (gx, lax.rem(gy + 1, GROUPS))
    south = (gx, lax.rem(gy + GROUPS - 1, GROUPS))

    barrier = pltpu.get_barrier_semaphore()
    for step in range(1, GROUPS):
        pl.semaphore_signal(barrier, inc=1, device_id=(gx, peer(step)), device_id_type=MESH)
    for side in (east, west):
        pl.semaphore_signal(barrier, inc=1, device_id=side, device_id_type=MESH)

    loads_in = [
        pltpu.make_async_copy(wgt, win, in_sem.at[0]),
        pltpu.make_async_copy(vel.at[pl.ds(0, CELLS)], v0.at[pl.ds(CY, CELLS)], in_sem.at[1]),
        pltpu.make_async_copy(vel.at[pl.ds(CELLS, CELLS)], v0.at[pl.ds(SPAN + CY, CELLS)], in_sem.at[2]),
        pltpu.make_async_copy(met, jac.at[pl.ds(CY, CELLS)], in_sem.at[3]),
    ]
    for copy in loads_in:
        copy.start()

    chunks = FACES // NZ
    tile = tile_ref[...]
    away = (((tile // SIDE) - mz + SIDE) % SIDE) * SIDE + ((tile % SIDE) - mx + SIDE) % SIDE
    member = jnp.concatenate([(away == t).astype(f32) for t in range(GROUPS)], axis=0)
    member16 = member.astype(bf16)
    upto = (iota((NZ, NZ), 0) <= iota((NZ, NZ), 1)).astype(f32).astype(bf16)
    rows_i = iota((GROUPS * chunks, GROUPS * chunks), 0)
    cols_i = iota((GROUPS * chunks, GROUPS * chunks), 1)
    ahead = ((rows_i // chunks == cols_i // chunks) & (cols_i < rows_i)).astype(f32).astype(bf16)
    ones = jnp.ones((2 * NZ, NZ), bf16)
    earlier = mm(mm(ahead, member16).astype(bf16), ones[:NZ])
    rank = mm(member16, upto) + earlier
    position = jnp.zeros((chunks, NZ), f32)
    for t in range(GROUPS):
        sl = slice(t * chunks, (t + 1) * chunks)
        position = position + member[sl] * (rank[sl] + (t * CAP - 1.0))
    position = position.astype(i32)
    hi = position // NZ
    lo = position % NZ
    hi_face[...] = hi
    lo_face[...] = lo
    cell = cell_ref[...]
    cell_hi = (cell // NZ + 1).astype(f32)
    cell_lo = (cell % NZ).astype(f32)
    r1, r2, r3 = thirds(rey_ref[...])
    r1, r2, r3 = r1.astype(f32), r2.astype(f32), r3.astype(f32)
    lane_row = iota((1, NZ), 1).astype(f32)
    for ch in range(chunks):
        one = slice(ch, ch + 1)
        span = slice(ch * NZ, (ch + 1) * NZ)
        b_face[:, span] = (iota((NZ, NZ), 0) == lo[one]).astype(f32).astype(bf16)
        mask = iota((2 * GROUPS, NZ), 0) == hi[one]
        values = [
            jnp.full((1, NZ), float(ch), f32), lane_row, cell_hi[one], cell_lo[one], r1[one], r2[one], r3[one],
        ]
        a_face[:, span] = jnp.concatenate([jnp.where(mask, v, 0.0) for v in values], axis=0).astype(bf16)
    table = mm_nt(a_face[...], b_face[...])
    part = [table[q * 2 * GROUPS : (q + 1) * 2 * GROUPS] for q in range(7)]
    inv_v[...] = jnp.clip((part[0] * float(NZ) + part[1]).astype(i32), 0, FACES - 1)
    slot_cell = jnp.where(part[2] > 0.0, (part[2] - 1.0) * float(NZ) + part[3], -1.0)
    slot_rey = (part[4] + part[5]) + part[6]
    to_smem = pltpu.make_async_copy(inv_v, inv_s, smem_sem.at[0])
    to_smem.start()
    blank = jnp.zeros((4, NZ), f32)
    for step in range(GROUPS):
        two = slice(step * HALF, (step + 1) * HALF)
        msend[step] = jnp.concatenate([slot_cell[two], slot_rey[two], blank], axis=0)

    pl.semaphore_wait(barrier, GROUPS + 1)

    def meta_copy(step):
        return pltpu.make_async_remote_copy(
            src_ref=msend.at[step], dst_ref=mrecv.at[step],
            send_sem=ms_sem.at[step], recv_sem=mr_sem.at[step],
            device_id=(gx, peer(step)), device_id_type=MESH,
        )

    def weight_copy(step):
        return pltpu.make_async_remote_copy(
            src_ref=wsend.at[pl.ds(step * CAP, CAP)], dst_ref=wrecv.at[pl.ds(step * CAP, CAP)],
            send_sem=ws_sem.at[step], recv_sem=wr_sem.at[step],
            device_id=(gx, peer(step)), device_id_type=MESH,
        )

    def stress_copy(step):
        return pltpu.make_async_remote_copy(
            src_ref=rsend.at[step], dst_ref=rrecv.at[step],
            send_sem=rs_sem.at[step], recv_sem=rr_sem.at[step],
            device_id=(gx, peer(GROUPS - step if step % SIDE == 0 else GROUPS - step + SIDE)),
            device_id_type=MESH,
        )

    for step in range(1, GROUPS):
        meta_copy(step).start()

    to_smem.wait()
    loads_in[0].wait()

    def pack(step):
        def some(g, carry):
            for u in range(16):
                slot = g * 16 + u
                face = inv_s[step * HALF + g // 8, (g % 8) * 16 + u]
                wsend[pl.ds(step * CAP + slot, 1), :] = win[pl.ds(face, 1), :]
            return carry

        lax.fori_loop(0, CAP // 16, some, 0)

    def pack_send(step, carry):
        pack(step)
        weight_copy(step).start()
        return carry

    lax.fori_loop(1, GROUPS, pack_send, 0)
    pack(0)

    for copy in loads_in[1:]:
        copy.wait()

    def edges(buffer, jacobian, x_edge, y_edge):
        for n, at in enumerate((CY, CX * CY)):
            for c in range(2):
                x_edge[n, pl.ds(c * CY, CY), :] = buffer[pl.ds(c * SPAN + at, CY), :]
            if jacobian is not None:
                x_edge[n, pl.ds(2 * CY, CY), :] = jacobian[pl.ds(at, CY), :]
        for n, at in enumerate((CY, CY + CY - 1)):
            for c in range(2):
                y_edge[n, pl.ds(c * CX, CX), :] = buffer[pl.ds(c * SPAN + at, CX, stride=CY), :]
            if jacobian is not None:
                y_edge[n, pl.ds(2 * CX, CX), :] = jacobian[pl.ds(at, CX, stride=CY), :]

    def halo_copies(x_edge, y_edge, x_halo, y_halo, base):
        made = []
        for n, (edge, halo, way, device) in enumerate((
            (x_edge, x_halo, 0, west), (x_edge, x_halo, 1, east),
            (y_edge, y_halo, 0, south), (y_edge, y_halo, 1, north),
        )):
            made.append(pltpu.make_async_remote_copy(
                src_ref=edge.at[way], dst_ref=halo.at[way],
                send_sem=hs_sem.at[base + n], recv_sem=hr_sem.at[base + n],
                device_id=device, device_id_type=MESH,
            ))
        return made

    edges(v0, jac, ex, ey)
    halos = halo_copies(ex, ey, hx, hy, 0)
    for copy in halos:
        copy.start()

    mine[...] = msend[0]
    for step in range(GROUPS):
        two = slice(step * HALF, (step + 1) * HALF)
        if step:
            meta_copy(step).wait_recv()
            block = mrecv[step]
        else:
            block = mine[...]
        meta_cell[two, :] = block[0:HALF]
        meta_rey[two, :] = block[HALF : 2 * HALF]
    slot_of = meta_cell[...].astype(i32)
    cell_v[...] = jnp.clip(slot_of, 0, CELLS - 1) * 4
    cells_smem = pltpu.make_async_copy(cell_v, cell_s, smem_sem.at[1])
    cells_smem.start()
    used = slot_of >= 0
    s_hi = jnp.where(used, slot_of // NZ, -1)
    s_lo = jnp.where(used, slot_of % NZ, -1)
    for j in range(2 * GROUPS):
        b_slot[:, j * NZ : (j + 1) * NZ] = (iota((NZ, NZ), 0) == s_lo[j : j + 1]).astype(f32).astype(bf16)

    for copy in halos:
        copy.wait_recv()

    row_y = iota((CY, NZ), 0)
    lane = iota((CY, NZ), 1)
    at_first, at_last = row_y == 0, row_y == CY - 1
    top, bottom = lane == NZ - 1, lane == 0

    for c in range(2):
        v0[pl.ds(c * SPAN + (CX + 1) * CY, CY), :] = hx[0, pl.ds(c * CY, CY), :]
        v0[pl.ds(c * SPAN, CY), :] = hx[1, pl.ds(c * CY, CY), :]
    jac[pl.ds((CX + 1) * CY, CY), :] = hx[0, pl.ds(2 * CY, CY), :]
    jac[pl.ds(0, CY), :] = hx[1, pl.ds(2 * CY, CY), :]

    def star(buffer, base, halo, row, x):
        at = pl.multiple_of(base + (x + 1) * CY, CY)
        centre = buffer[pl.ds(at, CY), :]
        next_x = buffer[pl.ds(pl.multiple_of(at + CY, CY), CY), :]
        last_x = buffer[pl.ds(pl.multiple_of(at - CY, CY), CY), :]
        next_y = pltpu.roll(centre, CY - 1, 0)
        last_y = pltpu.roll(centre, 1, 0)
        next_y = jnp.where(at_last, halo[0, pl.ds(row + x, 1), :], next_y)
        last_y = jnp.where(at_first, halo[1, pl.ds(row + x, 1), :], last_y)
        return centre, next_x, last_x, next_y, last_y

    def advance(buffer, halo, x):
        j, j_e, j_w, j_n, j_s = star(jac, 0, hy, 2 * CX, x)
        inverse = 1.0 / j
        k_e, k_w, k_n, k_s = j + j_e, j + j_w, j + j_n, j + j_s
        k_h = (time_step * viscosity * 0.5) * inverse
        k_v = (time_step * viscosity) * inverse * inverse
        stars = [star(buffer, c * SPAN, halo, c * CX, x) for c in range(2)]
        along = (-0.5 * time_step) * stars[0][0]
        across = (-0.5 * time_step) * stars[1][0]
        results = []
        for c in range(2):
            v, e, w, n, s = stars[c]
            spread = k_e * (e - v) + k_w * (w - v) + k_n * (n - v) + k_s * (s - v)
            above = jnp.where(top, 0.0, pltpu.roll(v, NZ - 1, 1))
            below = jnp.where(bottom, 0.0, pltpu.roll(v, 1, 1))
            change = along * (e - w) + across * (n - s) + k_h * spread + k_v * (above + below - 2.0 * v)
            results.append((v, change))
        return results

    def first_step(x, carry):
        for c, (v, change) in enumerate(advance(v0, hy, x)):
            new = v + change
            v1[pl.ds(pl.multiple_of(c * SPAN + (x + 1) * CY, CY), CY), :] = new
            cols[pl.ds(x * (4 * CY) + c, CY, stride=4), :] = v
            cols[pl.ds(x * (4 * CY) + 2 + c, CY, stride=4), :] = new
        return carry

    lax.fori_loop(0, CX, first_step, 0)

    cells_smem.wait()
    diagonal = iota((NZ, NZ), 0) == iota((NZ, NZ), 1)
    profile = prof_ref[...]

    def chunk(step, source):
        def some(g, carry):
            for u in range(16):
                slot = g * 16 + u
                where = cell_s[step * HALF + g // 8, (g % 8) * 16 + u]
                picked[pl.ds(slot * 4, 4), :] = cols[pl.ds(where, 4), :]
            return carry

        lax.fori_loop(0, CAP // 16, some, 0)
        weights = source[pl.ds(pl.multiple_of(step * CAP, CAP), CAP), :]
        for q in range(5):
            if q < 4:
                product = picked[pl.ds(q, CAP, stride=4), :] * weights
            else:
                product = weights * profile
            for half, row in enumerate(row_sums(product, ones, diagonal)):
                dots[q, pl.ds(step * HALF + half, 1), :] = row

    chunk(0, wsend)

    def arrived(step, carry):
        weight_copy(step).wait_recv()
        chunk(step, wrecv)
        return carry

    lax.fori_loop(1, GROUPS, arrived, 0)

    reynolds = meta_rey[...]

    def load_of(stress):
        pieces = [thirds(jnp.where(used, s, 0.0)) for s in stress]
        pieces = [[p.astype(f32) for p in piece] for piece in pieces]
        for j in range(2 * GROUPS):
            one = slice(j, j + 1)
            mask = iota((GROUPS, NZ), 0) == s_hi[one]
            parts = [jnp.where(mask, pieces[c][k][one], 0.0) for k in range(3) for c in range(2)]
            parts.append(jnp.zeros((2 * GROUPS, NZ), f32))
            a_slot[:, j * NZ : (j + 1) * NZ] = jnp.concatenate(parts, axis=0).astype(bf16)
        total = mm_nt(b_slot[...], a_slot[...])
        return total + pltpu.roll(total, NZ - 2 * GROUPS, 1) + pltpu.roll(total, NZ - 4 * GROUPS, 1)

    stress = wall_stress(dots[0], dots[1], reynolds)
    load = load_of(stress)
    for c in range(2):
        for block in range(CELLS // NZ):
            at = pl.ds(c * SPAN + CY + block * NZ, NZ)
            column = c * GROUPS + block
            v1[at, :] = v1[at, :] - load[:, column : column + 1] * profile

    edges(v1, None, ex2, ey2)
    halos2 = halo_copies(ex2, ey2, hx2, hy2, 4)
    for copy in halos2:
        copy.start()

    by_column = jnp.transpose(load)[0 : 2 * GROUPS]
    pieces = thirds(by_column)
    for j in range(2 * GROUPS):
        seen = b_slot[:, j * NZ : (j + 1) * NZ]
        spread = mm(pieces[0], seen) + mm(pieces[1], seen) + mm(pieces[2], seen)
        mask = iota((GROUPS, NZ), 0) == s_hi[j : j + 1]
        for c in range(2):
            at_face = jnp.where(mask, spread[c * GROUPS : (c + 1) * GROUPS], 0.0)
            loads[c, j : j + 1, :] = jnp.sum(at_face, axis=0, keepdims=True)
    stress = wall_stress(dots[2] - loads[0] * dots[4], dots[3] - loads[1] * dots[4], reynolds)
    for step in range(GROUPS):
        two = slice(step * HALF, (step + 1) * HALF)
        rsend[step] = jnp.concatenate([stress[0][two], stress[1][two], blank], axis=0)
    for step in range(1, GROUPS):
        stress_copy(step).start()

    load = load_of(stress)
    for c in range(2):
        for block in range(CELLS // NZ):
            at = pl.ds(c * SPAN + CY + block * NZ, NZ)
            column = c * GROUPS + block
            vout[pl.ds(c * CELLS + block * NZ, NZ), :] = v1[at, :] - load[:, column : column + 1] * profile

    for copy in halos2:
        copy.wait_recv()
    for c in range(2):
        v1[pl.ds(c * SPAN + (CX + 1) * CY, CY), :] = hx2[0, pl.ds(c * CY, CY), :]
        v1[pl.ds(c * SPAN, CY), :] = hx2[1, pl.ds(c * CY, CY), :]

    quarter = CX // 4
    stores = []
    for k in range(4):
        def second_step(x, carry):
            for c, (v, change) in enumerate(advance(v1, hy2, x)):
                at = pl.ds(pl.multiple_of(c * CELLS + x * CY, CY), CY)
                vout[at, :] = vout[at, :] + change
            return carry

        lax.fori_loop(k * quarter, (k + 1) * quarter, second_step, 0)
        for c in range(2):
            at = pl.ds(c * CELLS + k * quarter * CY, quarter * CY)
            copy = pltpu.make_async_copy(vout.at[at], out.at[at], out_sem.at[2 * k + c])
            copy.start()
            stores.append(copy)

    mine[...] = rsend[0]
    for step in range(1, GROUPS):
        stress_copy(step).wait_recv()
    back = jnp.concatenate([mine[...]] + [rrecv[step] for step in range(1, GROUPS)], axis=0)
    pieces = thirds(back)
    for ch in range(chunks):
        one = slice(ch, ch + 1)
        span = slice(ch * NZ, (ch + 1) * NZ)
        seen = b_face[:, span]
        spread = mm(pieces[0], seen) + mm(pieces[1], seen) + mm(pieces[2], seen)
        place = hi_face[one, :]
        row = (place // HALF) * 8 + place % HALF
        for c in range(2):
            mask = iota((8 * GROUPS, NZ), 0) == row + c * HALF
            stress_out[c : c + 1, span] = jnp.sum(jnp.where(mask, spread, 0.0), axis=0, keepdims=True)

    for copy in stores:
        copy.wait()
    for copy in halos + halos2:
        copy.wait_send()
    for step in range(1, GROUPS):
        meta_copy(step).wait_send()
        weight_copy(step).wait_send()
        stress_copy(step).wait_send()


def local(velocity, metric, weights, reynolds, face_tile, face_cell, profile):
    vm = pltpu.VMEM
    dma = pltpu.SemaphoreType.DMA
    small = (FACES // NZ, NZ)
    scratch = [
        vm((2 * SPAN, NZ), f32), vm((2 * SPAN, NZ), f32), vm((SPAN, NZ), f32), vm((FACES, NZ), f32),
        vm((SLOTS, NZ), f32), vm((SLOTS, NZ), f32),
        vm((GROUPS, 8, NZ), f32), vm((GROUPS, 8, NZ), f32), vm((8, NZ), f32),
        vm(small, i32), vm(small, i32), vm((14 * GROUPS, FACES), bf16), vm((NZ, FACES), bf16),
        vm((2 * GROUPS, NZ), f32), vm((2 * GROUPS, NZ), f32),
        vm((2 * GROUPS, NZ), i32), pltpu.SMEM((2 * GROUPS, NZ), i32),
        vm((2 * GROUPS, NZ), i32), pltpu.SMEM((2 * GROUPS, NZ), i32),
        vm((4 * CELLS + 8, NZ), f32), vm((4 * CAP + 8, NZ), f32), vm((5, 2 * GROUPS, NZ), f32),
        vm((NZ, SLOTS), bf16), vm((NZ, SLOTS), bf16), vm((2, 2 * GROUPS, NZ), f32),
        vm((2, 3 * CY, NZ), f32), vm((2, 3 * CX, NZ), f32), vm((2, 2 * CY, NZ), f32), vm((2, 2 * CX, NZ), f32),
        vm((2, 3 * CY, NZ), f32), vm((2, 3 * CX, NZ), f32), vm((2, 2 * CY, NZ), f32), vm((2, 2 * CX, NZ), f32),
        vm((2 * CELLS, NZ), f32), vm((GROUPS, 8, NZ), f32), vm((GROUPS, 8, NZ), f32),
        dma((4,)), dma((2,)), dma((GROUPS,)), dma((GROUPS,)), dma((GROUPS,)), dma((GROUPS,)),
        dma((8,)), dma((8,)), dma((GROUPS,)), dma((GROUPS,)), dma((8,)),
    ]
    whole = pl.BlockSpec(memory_space=pl.ANY)
    inside = pl.BlockSpec(memory_space=pltpu.VMEM)
    out, stress = pl.pallas_call(
        kernel,
        out_shape=(
            jax.ShapeDtypeStruct((2 * CELLS, NZ), f32),
            jax.ShapeDtypeStruct((2, FACES), f32),
        ),
        in_specs=[whole, whole, whole, inside, inside, inside, inside],
        out_specs=(whole, inside),
        scratch_shapes=scratch,
        compiler_params=pltpu.CompilerParams(
            collective_id=0, has_side_effects=True, vmem_limit_bytes=48 * 1024 * 1024
        ),
    )(
        velocity.reshape(2 * CELLS, NZ), metric.reshape(CELLS, NZ), weights,
        reynolds.reshape(small), face_tile.reshape(small), face_cell.reshape(small), profile.reshape(1, NZ),
    )
    return out.reshape(2, CX, CY, NZ), stress


def solution(mesh):
    placed = (
        P(None, "gx", "gy", None),
        P("gx", "gy", None),
        P(("gx", "gy"), None),
        P(("gx", "gy")),
        P(("gx", "gy"), None),
        P(("gx", "gy")),
        P(),
    )
    return jax.shard_map(
        local,
        mesh=mesh,
        in_specs=placed,
        out_specs=(P(None, "gx", "gy", None), P(None, ("gx", "gy"))),
        check_vma=False,
    )
```

profile of v0, /device:TPU:0, one launch (start us, length us, event | category | flops | bytes accessed | tf_op | source)
XLA Modules:
  0.0 87.7 jit_solution(17950622204105700110)
XLA Ops:
  0.6 0.0 copy-start
  0.6 1.2 %copy-done = f32[64,32,128]{2,1,0:T(8,128)S(1)} copy-done((f32[64,32,128]{2,1,0:T(8,128)S(1)}, f32[64,32,128]{2,1,0:T(8,128)}, u32[]{:S(2)}) %copy-start) | copy-done | bytes 1048600
  1.9 0.0 copy-start.1
  1.9 1.2 %copy-done.1 = f32[2048,128]{1,0:T(8,128)S(1)} copy-done((f32[2048,128]{1,0:T(8,128)S(1)}, f32[2048,128]{1,0:T(8,128)}, u32[]{:S(2)}) %copy-start.1) | copy-done | bytes 1048600
  3.1 0.0 copy-start.2
  3.1 0.7 copy-done.2
  3.8 0.0 copy-start.3
  3.8 0.7 copy-done.3
  4.5 0.0 copy-start.4
  4.5 0.7 copy-done.4
  5.2 0.0 copy-start.5
  5.2 0.7 copy-done.5
  5.8 79.9 %shard_map.86 = (f32[4096,128]{1,0:T(8,128)S(1)}, f32[2,2048]{1,0:T(2,128)S(1)}) custom-call(f32[4096,128]{1,0:T(8,128)} %bitcast.13, f32[2048,128]{1,0:T(8,128)S(1)} %bitcast.8, f32[2048,128]{1,0:T(8,128)S(1)} %copy-done.1, f32[16,128]{1,0:T(8,128)S(1)} %bitcast.9, s32[16,128]{1,0:T(8,128)S(1)} %bitcast.10, s32[16,128]{1,0:T(8,128)S(1)} %bitcast.11, ...), custom_call_target="tpu_custom_call" | custom-call | tf_op jit(solution)/shard_map/pallas_call | solution.py:463
  85.8 1.3 %copy.11 = f32[2,64,32,128]{3,2,1,0:T(8,128)} copy(f32[2,64,32,128]{3,2,1,0:T(8,128)S(1)} %bitcast.7) | data formatting | bytes 4194304
  87.1 0.6 copy.12
Async XLA Ops:
  0.6 1.2 %copy-start = (f32[64,32,128]{2,1,0:T(8,128)S(1)}, f32[64,32,128]{2,1,0:T(8,128)}, u32[]{:S(2)}) copy-start(f32[64,32,128]{2,1,0:T(8,128)} %param.8) | copy-start | bytes 3145732
  1.9 1.2 %copy-start.1 = (f32[2048,128]{1,0:T(8,128)S(1)}, f32[2048,128]{1,0:T(8,128)}, u32[]{:S(2)}) copy-start(f32[2048,128]{1,0:T(8,128)} %wgt.1) | copy-start | bytes 3145732
  3.1 0.7 copy-start.2
  3.8 0.7 copy-start.3
  4.5 0.7 copy-start.4
  5.2 0.7 copy-start.5
where the time goes:
time: 88.1 us; the launch traced here: 87.7 us
  Pallas kernels  79.9 us (91%)
  local copies, waits for them, and re-layouts  7.11 us (8%)
    pallas_call x1, Pallas kernels, local(): pl.pallas_call(kernel, out_shape=(jax.ShapeDtypeStruct((2 * CELLS, NZ), f...  79.9 us
    unnamed x14, local copies, waits for them, and re-layouts  7.11 us

commit v1 on v0

--- a/solution.py
+++ b/solution.py
@@ -16,7 +16,7 @@
 SLOTS = GROUPS * CAP
 CELLS = CX * CY
 SPAN = (CX + 2) * CY
-HALF = CAP // NZ
+BLOCK = CAP // 8
 
 karman = 0.41
 time_step = 0.2
@@ -28,6 +28,8 @@
 i32 = jnp.int32
 
 NT = (((1,), (1,)), ((), ()))
+
+ORDER = (4, 12, 1, 3, 8, 2, 5, 15, 7, 13, 10, 6, 14, 9, 11)
 
 
 def iota(shape, dim):
@@ -50,14 +52,21 @@
     return first, second, third
 
 
-def row_sums(product, ones, diagonal):
-    first, second, third = thirds(product)
-    total = mm(jnp.concatenate([first, second], axis=1), ones) + mm(third, ones[:NZ])
-    rows = []
-    for half in range(HALF):
-        part = total[half * NZ : (half + 1) * NZ]
-        rows.append(jnp.sum(jnp.where(diagonal, part, 0.0), axis=0, keepdims=True))
-    return rows
+def fold(values, level):
+    n = values.shape[0]
+    gap = 1 << level
+    pair = values.reshape(n // 2, 2, 8, NZ)
+    first, second = pair[:, 0], pair[:, 1]
+    low = (iota((n // 2, 8, NZ), 2) & gap) == 0
+    kept = jnp.where(low, first, second)
+    moved = jnp.where(low, second, first).reshape(n * 4, NZ)
+    return kept + pltpu.roll(moved, NZ - gap, 1).reshape(n // 2, 8, NZ)
+
+
+def nth(index):
+    words = [sum(step << (4 * k) for k, step in enumerate(ORDER[h : h + 7])) for h in (0, 7, 14)]
+    word = jnp.where(index < 7, words[0], jnp.where(index < 14, words[1], words[2]))
+    return (word >> (4 * (index % 7))) & 15
 
 
 def wall_stress(m0, m1, reynolds):
@@ -70,12 +79,13 @@
 
 
 def kernel(
-    vel, met, wgt, rey_ref, tile_ref, cell_ref, prof_ref,
+    vel, met, wgt, rey_in, tile_in, cell_in, prof_in,
     out, stress_out,
-    v0, v1, jac, win, wsend, wrecv, msend, mrecv, mine, lo_face, hi_face, a_face, b_face,
+    v0, v1, jac, win, wsend, wrecv, msend, mrecv, lo_face, hi_face, a_face, b_face,
     meta_cell, meta_rey, cell_v, cell_s, inv_v, inv_s, cols, picked, dots, b_slot, a_slot, loads,
-    hx, hy, hx2, hy2, ex, ey, ex2, ey2, vout, rsend, rrecv,
-    in_sem, smem_sem, ms_sem, mr_sem, ws_sem, wr_sem, hs_sem, hr_sem, rs_sem, rr_sem, out_sem,
+    hx, hy, hx2, hy2, ex, ey, ex2, ey2, rsend, rrecv,
+    rey_ref, tile_ref, cell_ref, prof_ref,
+    in_sem, smem_sem, ms_sem, mr_sem, ws_sem, wr_sem, hs_sem, hr_sem, rs_sem, rr_sem,
 ):
     gx = lax.axis_index("gx")
     gy = lax.axis_index("gy")
@@ -97,6 +107,14 @@
     for side in (east, west):
         pl.semaphore_signal(barrier, inc=1, device_id=side, device_id_type=MESH)
 
+    small_in = [
+        pltpu.make_async_copy(tile_in, tile_ref, in_sem.at[4]),
+        pltpu.make_async_copy(cell_in, cell_ref, in_sem.at[5]),
+        pltpu.make_async_copy(rey_in, rey_ref, in_sem.at[6]),
+        pltpu.make_async_copy(prof_in, prof_ref, in_sem.at[7]),
+    ]
+    for copy in small_in:
+        copy.start()
     loads_in = [
         pltpu.make_async_copy(wgt, win, in_sem.at[0]),
         pltpu.make_async_copy(vel.at[pl.ds(0, CELLS)], v0.at[pl.ds(CY, CELLS)], in_sem.at[1]),
@@ -106,6 +124,8 @@
     for copy in loads_in:
         copy.start()
 
+    for copy in small_in:
+        copy.wait()
     chunks = FACES // NZ
     tile = tile_ref[...]
     away = (((tile // SIDE) - mz + SIDE) % SIDE) * SIDE + ((tile % SIDE) - mx + SIDE) % SIDE
@@ -118,13 +138,13 @@
     ones = jnp.ones((2 * NZ, NZ), bf16)
     earlier = mm(mm(ahead, member16).astype(bf16), ones[:NZ])
     rank = mm(member16, upto) + earlier
-    position = jnp.zeros((chunks, NZ), f32)
+    order = jnp.zeros((chunks, NZ), f32)
     for t in range(GROUPS):
         sl = slice(t * chunks, (t + 1) * chunks)
-        position = position + member[sl] * (rank[sl] + (t * CAP - 1.0))
-    position = position.astype(i32)
-    hi = position // NZ
-    lo = position % NZ
+        order = order + member[sl] * rank[sl]
+    order = order.astype(i32) - 1
+    hi = (away // SIDE) * 8 + order % 8
+    lo = (away % SIDE) * BLOCK + order // 8
     hi_face[...] = hi
     lo_face[...] = lo
     cell = cell_ref[...]
@@ -149,16 +169,13 @@
     slot_rey = (part[4] + part[5]) + part[6]
     to_smem = pltpu.make_async_copy(inv_v, inv_s, smem_sem.at[0])
     to_smem.start()
-    blank = jnp.zeros((4, NZ), f32)
-    for step in range(GROUPS):
-        two = slice(step * HALF, (step + 1) * HALF)
-        msend[step] = jnp.concatenate([slot_cell[two], slot_rey[two], blank], axis=0)
-
-    pl.semaphore_wait(barrier, GROUPS + 1)
+    for g in range(SIDE):
+        eight = slice(g * 8, (g + 1) * 8)
+        msend[g] = jnp.concatenate([slot_cell[eight], slot_rey[eight]], axis=0)
 
     def meta_copy(step):
         return pltpu.make_async_remote_copy(
-            src_ref=msend.at[step], dst_ref=mrecv.at[step],
+            src_ref=msend.at[step // SIDE], dst_ref=mrecv.at[step],
             send_sem=ms_sem.at[step], recv_sem=mr_sem.at[step],
             device_id=(gx, peer(step)), device_id_type=MESH,
         )
@@ -172,35 +189,39 @@
 
     def stress_copy(step):
         return pltpu.make_async_remote_copy(
-            src_ref=rsend.at[step], dst_ref=rrecv.at[step],
+            src_ref=rsend.at[step // SIDE], dst_ref=rrecv.at[step],
             send_sem=rs_sem.at[step], recv_sem=rr_sem.at[step],
             device_id=(gx, peer(GROUPS - step if step % SIDE == 0 else GROUPS - step + SIDE)),
             device_id_type=MESH,
         )
 
-    for step in range(1, GROUPS):
-        meta_copy(step).start()
-
-    to_smem.wait()
-    loads_in[0].wait()
-
     def pack(step):
         def some(g, carry):
+            rows = []
             for u in range(16):
-                slot = g * 16 + u
-                face = inv_s[step * HALF + g // 8, (g % 8) * 16 + u]
-                wsend[pl.ds(step * CAP + slot, 1), :] = win[pl.ds(face, 1), :]
+                face = inv_s[(step // SIDE) * 8 + u % 8, (step % SIDE) * BLOCK + g * 2 + u // 8]
+                rows.append(win[pl.ds(face, 1), :])
+            for u in range(16):
+                wsend[pl.ds(step * CAP + g * 16 + u, 1), :] = rows[u]
             return carry
 
         lax.fori_loop(0, CAP // 16, some, 0)
 
-    def pack_send(step, carry):
+    def pack_send(index, carry):
+        step = nth(index)
         pack(step)
         weight_copy(step).start()
         return carry
 
-    lax.fori_loop(1, GROUPS, pack_send, 0)
-    pack(0)
+    to_smem.wait()
+    loads_in[0].wait()
+    pack(ORDER[0])
+
+    pl.semaphore_wait(barrier, GROUPS + 1)
+    for step in ORDER:
+        meta_copy(step).start()
+    weight_copy(ORDER[0]).start()
+    lax.fori_loop(1, 4, pack_send, 0)
 
     for copy in loads_in[1:]:
         copy.wait()
@@ -235,16 +256,23 @@
     for copy in halos:
         copy.start()
 
-    mine[...] = msend[0]
-    for step in range(GROUPS):
-        two = slice(step * HALF, (step + 1) * HALF)
-        if step:
-            meta_copy(step).wait_recv()
-            block = mrecv[step]
-        else:
-            block = mine[...]
-        meta_cell[two, :] = block[0:HALF]
-        meta_rey[two, :] = block[HALF : 2 * HALF]
+    lax.fori_loop(4, GROUPS - 1, pack_send, 0)
+    pack(0)
+
+    for step in range(1, GROUPS):
+        meta_copy(step).wait_recv()
+    lanes16 = iota((16, NZ), 1) // BLOCK
+
+    def four(first, received, g):
+        rows = first if g == 0 else received[g * SIDE]
+        for k in range(1, SIDE):
+            rows = jnp.where(lanes16 == k, received[g * SIDE + k], rows)
+        return rows
+
+    for g in range(SIDE):
+        rows = four(msend[0], mrecv, g)
+        meta_cell[g * 8 : (g + 1) * 8, :] = rows[0:8]
+        meta_rey[g * 8 : (g + 1) * 8, :] = rows[8:16]
     slot_of = meta_cell[...].astype(i32)
     cell_v[...] = jnp.clip(slot_of, 0, CELLS - 1) * 4
     cells_smem = pltpu.make_async_copy(cell_v, cell_s, smem_sem.at[1])
@@ -274,8 +302,8 @@
         centre = buffer[pl.ds(at, CY), :]
         next_x = buffer[pl.ds(pl.multiple_of(at + CY, CY), CY), :]
         last_x = buffer[pl.ds(pl.multiple_of(at - CY, CY), CY), :]
-        next_y = pltpu.roll(centre, CY - 1, 0)
-        last_y = pltpu.roll(centre, 1, 0)
+        next_y = buffer[pl.ds(at + 1, CY), :]
+        last_y = buffer[pl.ds(at - 1, CY), :]
         next_y = jnp.where(at_last, halo[0, pl.ds(row + x, 1), :], next_y)
         last_y = jnp.where(at_first, halo[1, pl.ds(row + x, 1), :], last_y)
         return centre, next_x, last_x, next_y, last_y
@@ -310,15 +338,16 @@
     lax.fori_loop(0, CX, first_step, 0)
 
     cells_smem.wait()
-    diagonal = iota((NZ, NZ), 0) == iota((NZ, NZ), 1)
     profile = prof_ref[...]
 
     def chunk(step, source):
         def some(g, carry):
+            rows = []
             for u in range(16):
-                slot = g * 16 + u
-                where = cell_s[step * HALF + g // 8, (g % 8) * 16 + u]
-                picked[pl.ds(slot * 4, 4), :] = cols[pl.ds(where, 4), :]
+                where = cell_s[(step // SIDE) * 8 + u % 8, (step % SIDE) * BLOCK + g * 2 + u // 8]
+                rows.append(cols[pl.ds(where, 4), :])
+            for u in range(16):
+                picked[pl.ds((g * 16 + u) * 4, 4), :] = rows[u]
             return carry
 
         lax.fori_loop(0, CAP // 16, some, 0)
@@ -328,17 +357,22 @@
                 product = picked[pl.ds(q, CAP, stride=4), :] * weights
             else:
                 product = weights * profile
-            for half, row in enumerate(row_sums(product, ones, diagonal)):
-                dots[q, pl.ds(step * HALF + half, 1), :] = row
+            product = product.reshape(BLOCK, 8, NZ)
+            for level in range(5):
+                product = fold(product, level)
+            dots[pl.ds(q * GROUPS + step, 1)] = product
 
     chunk(0, wsend)
 
-    def arrived(step, carry):
+    def arrived(index, carry):
+        step = nth(index)
         weight_copy(step).wait_recv()
         chunk(step, wrecv)
         return carry
 
-    lax.fori_loop(1, GROUPS, arrived, 0)
+    lax.fori_loop(0, GROUPS - 1, arrived, 0)
+    sums = fold(fold(dots[...], 5), 6)
+    sums = [sums[q * SIDE : (q + 1) * SIDE].reshape(2 * GROUPS, NZ) for q in range(5)]
 
     reynolds = meta_rey[...]
 
@@ -354,7 +388,7 @@
         total = mm_nt(b_slot[...], a_slot[...])
         return total + pltpu.roll(total, NZ - 2 * GROUPS, 1) + pltpu.roll(total, NZ - 4 * GROUPS, 1)
 
-    stress = wall_stress(dots[0], dots[1], reynolds)
+    stress = wall_stress(sums[0], sums[1], reynolds)
     load = load_of(stress)
     for c in range(2):
         for block in range(CELLS // NZ):
@@ -376,10 +410,10 @@
         for c in range(2):
             at_face = jnp.where(mask, spread[c * GROUPS : (c + 1) * GROUPS], 0.0)
             loads[c, j : j + 1, :] = jnp.sum(at_face, axis=0, keepdims=True)
-    stress = wall_stress(dots[2] - loads[0] * dots[4], dots[3] - loads[1] * dots[4], reynolds)
-    for step in range(GROUPS):
-        two = slice(step * HALF, (step + 1) * HALF)
-        rsend[step] = jnp.concatenate([stress[0][two], stress[1][two], blank], axis=0)
+    stress = wall_stress(sums[2] - loads[0] * sums[4], sums[3] - loads[1] * sums[4], reynolds)
+    for g in range(SIDE):
+        eight = slice(g * 8, (g + 1) * 8)
+        rsend[g] = jnp.concatenate([stress[0][eight], stress[1][eight]], axis=0)
     for step in range(1, GROUPS):
         stress_copy(step).start()
 
@@ -388,7 +422,7 @@
         for block in range(CELLS // NZ):
             at = pl.ds(c * SPAN + CY + block * NZ, NZ)
             column = c * GROUPS + block
-            vout[pl.ds(c * CELLS + block * NZ, NZ), :] = v1[at, :] - load[:, column : column + 1] * profile
+            out[pl.ds(c * CELLS + block * NZ, NZ), :] = v1[at, :] - load[:, column : column + 1] * profile
 
     for copy in halos2:
         copy.wait_recv()
@@ -396,26 +430,17 @@
         v1[pl.ds(c * SPAN + (CX + 1) * CY, CY), :] = hx2[0, pl.ds(c * CY, CY), :]
         v1[pl.ds(c * SPAN, CY), :] = hx2[1, pl.ds(c * CY, CY), :]
 
-    quarter = CX // 4
-    stores = []
-    for k in range(4):
-        def second_step(x, carry):
-            for c, (v, change) in enumerate(advance(v1, hy2, x)):
-                at = pl.ds(pl.multiple_of(c * CELLS + x * CY, CY), CY)
-                vout[at, :] = vout[at, :] + change
-            return carry
-
-        lax.fori_loop(k * quarter, (k + 1) * quarter, second_step, 0)
-        for c in range(2):
-            at = pl.ds(c * CELLS + k * quarter * CY, quarter * CY)
-            copy = pltpu.make_async_copy(vout.at[at], out.at[at], out_sem.at[2 * k + c])
-            copy.start()
-            stores.append(copy)
-
-    mine[...] = rsend[0]
+    def second_step(x, carry):
+        for c, (v, change) in enumerate(advance(v1, hy2, x)):
+            at = pl.ds(pl.multiple_of(c * CELLS + x * CY, CY), CY)
+            out[at, :] = out[at, :] + change
+        return carry
+
+    lax.fori_loop(0, CX, second_step, 0)
+
     for step in range(1, GROUPS):
         stress_copy(step).wait_recv()
-    back = jnp.concatenate([mine[...]] + [rrecv[step] for step in range(1, GROUPS)], axis=0)
+    back = jnp.concatenate([four(rsend[0], rrecv, g) for g in range(SIDE)], axis=0)
     pieces = thirds(back)
     for ch in range(chunks):
         one = slice(ch, ch + 1)
@@ -423,13 +448,11 @@
         seen = b_face[:, span]
         spread = mm(pieces[0], seen) + mm(pieces[1], seen) + mm(pieces[2], seen)
         place = hi_face[one, :]
-        row = (place // HALF) * 8 + place % HALF
+        row = (place // 8) * 16 + place % 8
         for c in range(2):
-            mask = iota((8 * GROUPS, NZ), 0) == row + c * HALF
+            mask = iota((SIDE * 16, NZ), 0) == row + c * 8
             stress_out[c : c + 1, span] = jnp.sum(jnp.where(mask, spread, 0.0), axis=0, keepdims=True)
 
-    for copy in stores:
-        copy.wait()
     for copy in halos + halos2:
         copy.wait_send()
     for step in range(1, GROUPS):
@@ -445,20 +468,21 @@
     scratch = [
         vm((2 * SPAN, NZ), f32), vm((2 * SPAN, NZ), f32), vm((SPAN, NZ), f32), vm((FACES, NZ), f32),
         vm((SLOTS, NZ), f32), vm((SLOTS, NZ), f32),
-        vm((GROUPS, 8, NZ), f32), vm((GROUPS, 8, NZ), f32), vm((8, NZ), f32),
+        vm((SIDE, 16, NZ), f32), vm((GROUPS, 16, NZ), f32),
         vm(small, i32), vm(small, i32), vm((14 * GROUPS, FACES), bf16), vm((NZ, FACES), bf16),
         vm((2 * GROUPS, NZ), f32), vm((2 * GROUPS, NZ), f32),
         vm((2 * GROUPS, NZ), i32), pltpu.SMEM((2 * GROUPS, NZ), i32),
         vm((2 * GROUPS, NZ), i32), pltpu.SMEM((2 * GROUPS, NZ), i32),
-        vm((4 * CELLS + 8, NZ), f32), vm((4 * CAP + 8, NZ), f32), vm((5, 2 * GROUPS, NZ), f32),
+        vm((4 * CELLS + 8, NZ), f32), vm((4 * CAP + 8, NZ), f32), vm((5 * GROUPS, 8, NZ), f32),
         vm((NZ, SLOTS), bf16), vm((NZ, SLOTS), bf16), vm((2, 2 * GROUPS, NZ), f32),
         vm((2, 3 * CY, NZ), f32), vm((2, 3 * CX, NZ), f32), vm((2, 2 * CY, NZ), f32), vm((2, 2 * CX, NZ), f32),
         vm((2, 3 * CY, NZ), f32), vm((2, 3 * CX, NZ), f32), vm((2, 2 * CY, NZ), f32), vm((2, 2 * CX, NZ), f32),
-        vm((2 * CELLS, NZ), f32), vm((GROUPS, 8, NZ), f32), vm((GROUPS, 8, NZ), f32),
-        dma((4,)), dma((2,)), dma((GROUPS,)), dma((GROUPS,)), dma((GROUPS,)), dma((GROUPS,)),
-        dma((8,)), dma((8,)), dma((GROUPS,)), dma((GROUPS,)), dma((8,)),
+        vm((SIDE, 16, NZ), f32), vm((GROUPS, 16, NZ), f32),
+        vm(small, f32), vm(small, i32), vm(small, i32), vm((1, NZ), f32),
+        dma((8,)), dma((2,)), dma((GROUPS,)), dma((GROUPS,)), dma((GROUPS,)), dma((GROUPS,)),
+        dma((8,)), dma((8,)), dma((GROUPS,)), dma((GROUPS,)),
     ]
-    whole = pl.BlockSpec(memory_space=pl.ANY)
+    whole = pl.BlockSpec(memory_space=pltpu.HBM)
     inside = pl.BlockSpec(memory_space=pltpu.VMEM)
     out, stress = pl.pallas_call(
         kernel,
@@ -466,8 +490,8 @@
             jax.ShapeDtypeStruct((2 * CELLS, NZ), f32),
             jax.ShapeDtypeStruct((2, FACES), f32),
         ),
-        in_specs=[whole, whole, whole, inside, inside, inside, inside],
-        out_specs=(whole, inside),
+        in_specs=[whole] * 7,
+        out_specs=(inside, inside),
         scratch_shapes=scratch,
         compiler_params=pltpu.CompilerParams(
             collective_id=0, has_side_effects=True, vmem_limit_bytes=48 * 1024 * 1024

time: 88.1 us -> 64.2 us (0.73)
  Pallas kernels: 79.9 us -> 56.1 us
    pallas_call x1, Pallas kernels: 79.9 us -> 56.1 us  [local(): pl.pallas_call(kernel, out_shape=(jax.ShapeDtypeStruct((2 * CELLS, NZ), f...]
where the time goes in v1:
time: 64.2 us; the launch traced here: 63.9 us
  Pallas kernels  56.1 us (87%)
  local copies, waits for them, and re-layouts  7.11 us (11%)
  between operations  0.65 us (1%)
    pallas_call x1, Pallas kernels, local(): pl.pallas_call(kernel, out_shape=(jax.ShapeDtypeStruct((2 * CELLS, NZ), f...  56.1 us
    unnamed x14, local copies, waits for them, and re-layouts  7.11 us

profile of v1, /device:TPU:0, one launch (start us, length us, event | category | flops | bytes accessed | tf_op | source)
XLA Modules:
  0.0 63.9 jit_solution(1251609476165481651)
XLA Ops:
  0.6 0.0 copy-start
  0.6 1.2 %copy-done = f32[64,32,128]{2,1,0:T(8,128)S(1)} copy-done((f32[64,32,128]{2,1,0:T(8,128)S(1)}, f32[64,32,128]{2,1,0:T(8,128)}, u32[]{:S(2)}) %copy-start) | copy-done | bytes 1048600
  1.9 0.0 copy-start.1
  1.9 1.2 %copy-done.1 = f32[2048,128]{1,0:T(8,128)S(1)} copy-done((f32[2048,128]{1,0:T(8,128)S(1)}, f32[2048,128]{1,0:T(8,128)}, u32[]{:S(2)}) %copy-start.1) | copy-done | bytes 1048600
  3.1 0.0 copy-start.2
  3.1 0.7 %copy-done.2 = f32[2048]{0:T(1024)S(1)} copy-done((f32[2048]{0:T(1024)S(1)}, f32[2048]{0:T(1024)}, u32[]{:S(2)}) %copy-start.2) | copy-done | bytes 8216
  3.8 0.0 copy-start.3
  3.8 0.7 %copy-done.3 = s32[2048,1]{0,1:T(1,128)S(1)} copy-done((s32[2048,1]{0,1:T(1,128)S(1)}, s32[2048,1]{0,1:T(1,128)}, u32[]{:S(2)}) %copy-start.3) | copy-done | bytes 8216
  4.5 0.0 copy-start.4
  4.5 0.7 %copy-done.4 = s32[2048]{0:T(1024)S(1)} copy-done((s32[2048]{0:T(1024)S(1)}, s32[2048]{0:T(1024)}, u32[]{:S(2)}) %copy-start.4) | copy-done | bytes 8216
  5.2 0.0 copy-start.5
  5.2 0.7 %copy-done.5 = f32[128]{0:T(128)S(1)} copy-done((f32[128]{0:T(128)S(1)}, f32[128]{0:T(128)}, u32[]{:S(2)}) %copy-start.5) | copy-done | bytes 536
  5.8 56.1 %shard_map.86 = (f32[4096,128]{1,0:T(8,128)S(1)}, f32[2,2048]{1,0:T(2,128)S(1)}) custom-call(f32[4096,128]{1,0:T(8,128)} %bitcast.13, f32[2048,128]{1,0:T(8,128)S(1)} %bitcast.8, f32[2048,128]{1,0:T(8,128)S(1)} %copy-done.1, f32[16,128]{1,0:T(8,128)S(1)} %bitcast.9, s32[16,128]{1,0:T(8,128)S(1)} %bitcast.10, s32[16,128]{1,0:T(8,128)S(1)} %bitcast.11, ...), custom_call_target="tpu_custom_call" | custom-call | tf_op jit(solution)/shard_map/pallas_call | solution.py:487
  61.9 1.3 %copy.11 = f32[2,64,32,128]{3,2,1,0:T(8,128)} copy(f32[2,64,32,128]{3,2,1,0:T(8,128)S(1)} %bitcast.7) | data formatting | bytes 4194304
  63.3 0.6 copy.12
Async XLA Ops:
  0.6 1.2 %copy-start = (f32[64,32,128]{2,1,0:T(8,128)S(1)}, f32[64,32,128]{2,1,0:T(8,128)}, u32[]{:S(2)}) copy-start(f32[64,32,128]{2,1,0:T(8,128)} %param.8) | copy-start | bytes 3145732
  1.9 1.2 %copy-start.1 = (f32[2048,128]{1,0:T(8,128)S(1)}, f32[2048,128]{1,0:T(8,128)}, u32[]{:S(2)}) copy-start(f32[2048,128]{1,0:T(8,128)} %wgt.1) | copy-start | bytes 3145732
  3.1 0.7 %copy-start.2 = (f32[2048]{0:T(1024)S(1)}, f32[2048]{0:T(1024)}, u32[]{:S(2)}) copy-start(f32[2048]{0:T(1024)} %param.10) | copy-start | bytes 24580
  3.8 0.7 %copy-start.3 = (s32[2048,1]{0,1:T(1,128)S(1)}, s32[2048,1]{0,1:T(1,128)}, u32[]{:S(2)}) copy-start(s32[2048,1]{0,1:T(1,128)} %param.11) | copy-start | bytes 24580
  4.5 0.7 %copy-start.4 = (s32[2048]{0:T(1024)S(1)}, s32[2048]{0:T(1024)}, u32[]{:S(2)}) copy-start(s32[2048]{0:T(1024)} %param.12) | copy-start | bytes 24580
  5.2 0.7 %copy-start.5 = (f32[128]{0:T(128)S(1)}, f32[128]{0:T(128)}, u32[]{:S(2)}) copy-start(f32[128]{0:T(128)} %param.13) | copy-start | bytes 1540

commit v2 on v1

--- a/solution.py
+++ b/solution.py
@@ -29,7 +29,7 @@
 
 NT = (((1,), (1,)), ((), ()))
 
-ORDER = (4, 12, 1, 3, 8, 2, 5, 15, 7, 13, 10, 6, 14, 9, 11)
+ORDER = (0, 4, 12, 1, 3, 8, 2, 5, 15, 7, 13, 10, 6, 14, 9, 11)
 
 
 def iota(shape, dim):
@@ -52,21 +52,10 @@
     return first, second, third
 
 
-def fold(values, level):
-    n = values.shape[0]
-    gap = 1 << level
-    pair = values.reshape(n // 2, 2, 8, NZ)
-    first, second = pair[:, 0], pair[:, 1]
-    low = (iota((n // 2, 8, NZ), 2) & gap) == 0
-    kept = jnp.where(low, first, second)
-    moved = jnp.where(low, second, first).reshape(n * 4, NZ)
-    return kept + pltpu.roll(moved, NZ - gap, 1).reshape(n // 2, 8, NZ)
-
-
 def nth(index):
-    words = [sum(step << (4 * k) for k, step in enumerate(ORDER[h : h + 7])) for h in (0, 7, 14)]
-    word = jnp.where(index < 7, words[0], jnp.where(index < 14, words[1], words[2]))
-    return (word >> (4 * (index % 7))) & 15
+    words = [sum(step << (4 * k) for k, step in enumerate(ORDER[h : h + 4])) for h in (0, 4, 8, 12)]
+    word = jnp.where(index < 8, jnp.where(index < 4, words[0], words[1]), jnp.where(index < 12, words[2], words[3]))
+    return (word >> (4 * (index % 4))) & 15
 
 
 def wall_stress(m0, m1, reynolds):
@@ -82,7 +71,7 @@
     vel, met, wgt, rey_in, tile_in, cell_in, prof_in,
     out, stress_out,
     v0, v1, jac, win, wsend, wrecv, msend, mrecv, lo_face, hi_face, a_face, b_face,
-    meta_cell, meta_rey, cell_v, cell_s, inv_v, inv_s, cols, picked, dots, b_slot, a_slot, loads,
+    meta_cell, meta_rey, cell_v, cell_s, inv_v, inv_s, cols, picked, dots, b_slot, b_rows, a_slot, so_far, factors, loads,
     hx, hy, hx2, hy2, ex, ey, ex2, ey2, rsend, rrecv,
     rey_ref, tile_ref, cell_ref, prof_ref,
     in_sem, smem_sem, ms_sem, mr_sem, ws_sem, wr_sem, hs_sem, hr_sem, rs_sem, rr_sem,
@@ -94,6 +83,13 @@
 
     def peer(step):
         return ((mz + step // SIDE) % SIDE) * SIDE + (mx + step % SIDE) % SIDE
+
+    def target(index):
+        return peer(ORDER[index] if isinstance(index, int) else nth(index))
+
+    def origin(index):
+        step = ORDER[index]
+        return peer(((SIDE - step // SIDE) % SIDE) * SIDE + (SIDE - step % SIDE) % SIDE)
 
     n_gx = lax.axis_size("gx")
     east = (lax.rem(gx + 1, n_gx), gy)
@@ -129,7 +125,7 @@
     chunks = FACES // NZ
     tile = tile_ref[...]
     away = (((tile // SIDE) - mz + SIDE) % SIDE) * SIDE + ((tile % SIDE) - mx + SIDE) % SIDE
-    member = jnp.concatenate([(away == t).astype(f32) for t in range(GROUPS)], axis=0)
+    member = jnp.concatenate([(away == step).astype(f32) for step in ORDER], axis=0)
     member16 = member.astype(bf16)
     upto = (iota((NZ, NZ), 0) <= iota((NZ, NZ), 1)).astype(f32).astype(bf16)
     rows_i = iota((GROUPS * chunks, GROUPS * chunks), 0)
@@ -139,12 +135,15 @@
     earlier = mm(mm(ahead, member16).astype(bf16), ones[:NZ])
     rank = mm(member16, upto) + earlier
     order = jnp.zeros((chunks, NZ), f32)
+    chunk_of = jnp.zeros((chunks, NZ), f32)
     for t in range(GROUPS):
         sl = slice(t * chunks, (t + 1) * chunks)
         order = order + member[sl] * rank[sl]
+        chunk_of = chunk_of + member[sl] * float(t)
     order = order.astype(i32) - 1
-    hi = (away // SIDE) * 8 + order % 8
-    lo = (away % SIDE) * BLOCK + order // 8
+    chunk_of = chunk_of.astype(i32)
+    hi = (chunk_of // SIDE) * 8 + order % 8
+    lo = (chunk_of % SIDE) * BLOCK + order // 8
     hi_face[...] = hi
     lo_face[...] = lo
     cell = cell_ref[...]
@@ -177,51 +176,49 @@
         return pltpu.make_async_remote_copy(
             src_ref=msend.at[step // SIDE], dst_ref=mrecv.at[step],
             send_sem=ms_sem.at[step], recv_sem=mr_sem.at[step],
-            device_id=(gx, peer(step)), device_id_type=MESH,
+            device_id=(gx, target(step)), device_id_type=MESH,
         )
 
     def weight_copy(step):
         return pltpu.make_async_remote_copy(
             src_ref=wsend.at[pl.ds(step * CAP, CAP)], dst_ref=wrecv.at[pl.ds(step * CAP, CAP)],
             send_sem=ws_sem.at[step], recv_sem=wr_sem.at[step],
-            device_id=(gx, peer(step)), device_id_type=MESH,
+            device_id=(gx, target(step)), device_id_type=MESH,
         )
 
     def stress_copy(step):
         return pltpu.make_async_remote_copy(
             src_ref=rsend.at[step // SIDE], dst_ref=rrecv.at[step],
             send_sem=rs_sem.at[step], recv_sem=rr_sem.at[step],
-            device_id=(gx, peer(GROUPS - step if step % SIDE == 0 else GROUPS - step + SIDE)),
+            device_id=(gx, origin(step)),
             device_id_type=MESH,
         )
 
+    def gather(table, step, source, rows, target, first):
+        where = table.at[pl.ds((step // SIDE) * 8, 8), pl.ds((step % SIDE) * BLOCK, BLOCK)]
+        for v in range(0, BLOCK, 4):
+            places = [(k % 8, v + k // 8) for k in range(32)]
+            runs = [source[pl.ds(where[place], rows), :] for place in places]
+            for k, run in enumerate(runs):
+                target[pl.ds(first + (v * 8 + k) * rows, rows), :] = run
+
     def pack(step):
-        def some(g, carry):
-            rows = []
-            for u in range(16):
-                face = inv_s[(step // SIDE) * 8 + u % 8, (step % SIDE) * BLOCK + g * 2 + u // 8]
-                rows.append(win[pl.ds(face, 1), :])
-            for u in range(16):
-                wsend[pl.ds(step * CAP + g * 16 + u, 1), :] = rows[u]
-            return carry
-
-        lax.fori_loop(0, CAP // 16, some, 0)
-
-    def pack_send(index, carry):
-        step = nth(index)
+        gather(inv_s, step, win, 1, wsend, step * CAP)
+
+    def pack_send(step, carry):
         pack(step)
         weight_copy(step).start()
         return carry
 
     to_smem.wait()
     loads_in[0].wait()
-    pack(ORDER[0])
+    pack(1)
 
     pl.semaphore_wait(barrier, GROUPS + 1)
-    for step in ORDER:
+    for step in range(1, GROUPS):
         meta_copy(step).start()
-    weight_copy(ORDER[0]).start()
-    lax.fori_loop(1, 4, pack_send, 0)
+    weight_copy(1).start()
+    lax.fori_loop(2, 5, pack_send, 0)
 
     for copy in loads_in[1:]:
         copy.wait()
@@ -256,7 +253,7 @@
     for copy in halos:
         copy.start()
 
-    lax.fori_loop(4, GROUPS - 1, pack_send, 0)
+    lax.fori_loop(5, GROUPS, pack_send, 0)
     pack(0)
 
     for step in range(1, GROUPS):
@@ -281,7 +278,9 @@
     s_hi = jnp.where(used, slot_of // NZ, -1)
     s_lo = jnp.where(used, slot_of % NZ, -1)
     for j in range(2 * GROUPS):
-        b_slot[:, j * NZ : (j + 1) * NZ] = (iota((NZ, NZ), 0) == s_lo[j : j + 1]).astype(f32).astype(bf16)
+        seen = (iota((NZ, NZ), 0) == s_lo[j : j + 1]).astype(f32)
+        b_slot[:, j * NZ : (j + 1) * NZ] = seen.astype(bf16)
+        b_rows[j * NZ : (j + 1) * NZ, :] = jnp.transpose(seen).astype(bf16)
 
     for copy in halos:
         copy.wait_recv()
@@ -308,145 +307,189 @@
         last_y = jnp.where(at_first, halo[1, pl.ds(row + x, 1), :], last_y)
         return centre, next_x, last_x, next_y, last_y
 
-    def advance(buffer, halo, x):
+    def column_sum(v):
+        above = jnp.where(top, 0.0, pltpu.roll(v, NZ - 1, 1))
+        below = jnp.where(bottom, 0.0, pltpu.roll(v, 1, 1))
+        return above + below
+
+    def first_step(x, carry):
         j, j_e, j_w, j_n, j_s = star(jac, 0, hy, 2 * CX, x)
         inverse = 1.0 / j
-        k_e, k_w, k_n, k_s = j + j_e, j + j_w, j + j_n, j + j_s
         k_h = (time_step * viscosity * 0.5) * inverse
         k_v = (time_step * viscosity) * inverse * inverse
-        stars = [star(buffer, c * SPAN, halo, c * CX, x) for c in range(2)]
+        k_e, k_w, k_n, k_s = k_h * (j + j_e), k_h * (j + j_w), k_h * (j + j_n), k_h * (j + j_s)
+        k_c = (k_e + k_w) + (k_n + k_s) + 2.0 * k_v
+        at = pl.ds(pl.multiple_of(x * CY, CY), CY)
+        for n, k in enumerate((k_e, k_w, k_n, k_s, k_v, k_c)):
+            factors[n, at, :] = k
+        stars = [star(v0, c * SPAN, hy, c * CX, x) for c in range(2)]
         along = (-0.5 * time_step) * stars[0][0]
         across = (-0.5 * time_step) * stars[1][0]
-        results = []
+        k_e, k_w, k_n, k_s = k_e + along, k_w - along, k_n + across, k_s - across
         for c in range(2):
             v, e, w, n, s = stars[c]
-            spread = k_e * (e - v) + k_w * (w - v) + k_n * (n - v) + k_s * (s - v)
-            above = jnp.where(top, 0.0, pltpu.roll(v, NZ - 1, 1))
-            below = jnp.where(bottom, 0.0, pltpu.roll(v, 1, 1))
-            change = along * (e - w) + across * (n - s) + k_h * spread + k_v * (above + below - 2.0 * v)
-            results.append((v, change))
-        return results
-
-    def first_step(x, carry):
-        for c, (v, change) in enumerate(advance(v0, hy, x)):
-            new = v + change
+            new = v + ((k_e * e + k_w * w) + (k_n * n + k_s * s) + (k_v * column_sum(v) - k_c * v))
             v1[pl.ds(pl.multiple_of(c * SPAN + (x + 1) * CY, CY), CY), :] = new
             cols[pl.ds(x * (4 * CY) + c, CY, stride=4), :] = v
             cols[pl.ds(x * (4 * CY) + 2 + c, CY, stride=4), :] = new
         return carry
 
+    def second_step(x, carry):
+        at = pl.ds(pl.multiple_of(x * CY, CY), CY)
+        k_e, k_w, k_n, k_s, k_v, k_c = [factors[n, at, :] for n in range(6)]
+        here = [pl.multiple_of(c * SPAN + (x + 1) * CY, CY) for c in range(2)]
+        centre = [v1[pl.ds(here[c], CY), :] for c in range(2)]
+        along = (-0.5 * time_step) * centre[0]
+        across = (-0.5 * time_step) * centre[1]
+        k_e, k_w = k_e + along, k_w - along
+        k_n = jnp.where(at_last, 0.0, k_n + across)
+        k_s = jnp.where(at_first, 0.0, k_s - across)
+        for c in range(2):
+            v = centre[c]
+            e = v1[pl.ds(pl.multiple_of(here[c] + CY, CY), CY), :]
+            w = v1[pl.ds(pl.multiple_of(here[c] - CY, CY), CY), :]
+            n = v1[pl.ds(here[c] + 1, CY), :]
+            s = v1[pl.ds(here[c] - 1, CY), :]
+            change = (k_e * e + k_w * w) + (k_n * n + k_s * s) + (k_v * column_sum(v) - k_c * v)
+            at = pl.ds(pl.multiple_of(c * CELLS + x * CY, CY), CY)
+            out[at, :] = out[at, :] + change
+        return carry
+
     lax.fori_loop(0, CX, first_step, 0)
 
     cells_smem.wait()
     profile = prof_ref[...]
 
+    lane8 = iota((8, NZ), 1) % BLOCK
+
     def chunk(step, source):
-        def some(g, carry):
-            rows = []
-            for u in range(16):
-                where = cell_s[(step // SIDE) * 8 + u % 8, (step % SIDE) * BLOCK + g * 2 + u // 8]
-                rows.append(cols[pl.ds(where, 4), :])
-            for u in range(16):
-                picked[pl.ds((g * 16 + u) * 4, 4), :] = rows[u]
-            return carry
-
-        lax.fori_loop(0, CAP // 16, some, 0)
+        gather(cell_s, step, cols, 4, picked, 0)
         weights = source[pl.ds(pl.multiple_of(step * CAP, CAP), CAP), :]
         for q in range(5):
             if q < 4:
                 product = picked[pl.ds(q, CAP, stride=4), :] * weights
             else:
                 product = weights * profile
-            product = product.reshape(BLOCK, 8, NZ)
-            for level in range(5):
-                product = fold(product, level)
-            dots[pl.ds(q * GROUPS + step, 1)] = product
-
-    chunk(0, wsend)
-
-    def arrived(index, carry):
-        step = nth(index)
+            total = jnp.sum(product, axis=1, keepdims=True)
+            rows = jnp.zeros((8, NZ), f32)
+            for v in range(BLOCK):
+                rows = jnp.where(lane8 == v, total[v * 8 : (v + 1) * 8], rows)
+            dots[pl.ds(q * GROUPS + step, 1)] = rows.reshape(1, 8, NZ)
+
+    def arrived(step, carry):
         weight_copy(step).wait_recv()
         chunk(step, wrecv)
         return carry
 
-    lax.fori_loop(0, GROUPS - 1, arrived, 0)
-    sums = fold(fold(dots[...], 5), 6)
-    sums = [sums[q * SIDE : (q + 1) * SIDE].reshape(2 * GROUPS, NZ) for q in range(5)]
+    lanes8 = iota((8, NZ), 1) // BLOCK
+
+    def group_sums(q, g):
+        rows = dots[q * GROUPS + g * SIDE]
+        for k in range(1, SIDE):
+            rows = jnp.where(lanes8 == k, dots[q * GROUPS + g * SIDE + k], rows)
+        return rows
+
+    def group_load(stress, g):
+        eight = slice(g * 8, (g + 1) * 8)
+        pieces = [[p.astype(f32) for p in thirds(jnp.where(used[eight], s, 0.0))] for s in stress]
+        for sub in range(8):
+            one = slice(sub, sub + 1)
+            mask = iota((GROUPS, NZ), 0) == s_hi[g * 8 + sub : g * 8 + sub + 1]
+            parts = [jnp.where(mask, pieces[c][k][one], 0.0) for k in range(3) for c in range(2)]
+            a_slot[:, sub * NZ : (sub + 1) * NZ] = jnp.concatenate(parts, axis=0).astype(bf16)
+        total = mm(a_slot[...], b_rows[g * 8 * NZ : (g + 1) * 8 * NZ, :])
+        width = 2 * GROUPS
+        return (total[0:width] + total[width : 2 * width]) + total[2 * width : 3 * width]
+
+    def by_cell(load):
+        return jnp.transpose(jnp.concatenate([load, jnp.zeros((NZ - 2 * GROUPS, NZ), f32)], axis=0))
 
     reynolds = meta_rey[...]
-
-    def load_of(stress):
-        pieces = [thirds(jnp.where(used, s, 0.0)) for s in stress]
-        pieces = [[p.astype(f32) for p in piece] for piece in pieces]
-        for j in range(2 * GROUPS):
-            one = slice(j, j + 1)
-            mask = iota((GROUPS, NZ), 0) == s_hi[one]
-            parts = [jnp.where(mask, pieces[c][k][one], 0.0) for k in range(3) for c in range(2)]
-            parts.append(jnp.zeros((2 * GROUPS, NZ), f32))
-            a_slot[:, j * NZ : (j + 1) * NZ] = jnp.concatenate(parts, axis=0).astype(bf16)
-        total = mm_nt(b_slot[...], a_slot[...])
-        return total + pltpu.roll(total, NZ - 2 * GROUPS, 1) + pltpu.roll(total, NZ - 4 * GROUPS, 1)
-
-    stress = wall_stress(sums[0], sums[1], reynolds)
-    load = load_of(stress)
+    load = None
+    for g in range(SIDE):
+        if g == 0:
+            chunk(0, wsend)
+        lax.fori_loop(max(1, g * SIDE), (g + 1) * SIDE, arrived, 0)
+        part = group_load(wall_stress(group_sums(0, g), group_sums(1, g), reynolds[g * 8 : (g + 1) * 8]), g)
+        if g < SIDE - 1:
+            so_far[...] = part if g == 0 else so_far[...] + part
+        else:
+            load = so_far[...] + part
+
+    spread = by_cell(load)
     for c in range(2):
         for block in range(CELLS // NZ):
             at = pl.ds(c * SPAN + CY + block * NZ, NZ)
             column = c * GROUPS + block
-            v1[at, :] = v1[at, :] - load[:, column : column + 1] * profile
+            v1[at, :] = v1[at, :] - spread[:, column : column + 1] * profile
 
     edges(v1, None, ex2, ey2)
     halos2 = halo_copies(ex2, ey2, hx2, hy2, 4)
     for copy in halos2:
         copy.start()
 
-    by_column = jnp.transpose(load)[0 : 2 * GROUPS]
-    pieces = thirds(by_column)
-    for j in range(2 * GROUPS):
-        seen = b_slot[:, j * NZ : (j + 1) * NZ]
-        spread = mm(pieces[0], seen) + mm(pieces[1], seen) + mm(pieces[2], seen)
-        mask = iota((GROUPS, NZ), 0) == s_hi[j : j + 1]
-        for c in range(2):
-            at_face = jnp.where(mask, spread[c * GROUPS : (c + 1) * GROUPS], 0.0)
-            loads[c, j : j + 1, :] = jnp.sum(at_face, axis=0, keepdims=True)
-    stress = wall_stress(sums[2] - loads[0] * sums[4], sums[3] - loads[1] * sums[4], reynolds)
+    pieces = jnp.concatenate(thirds(load), axis=0)
+    width = 2 * GROUPS
+    for g in range(SIDE):
+        seen = mm(pieces, b_slot[:, g * 8 * NZ : (g + 1) * 8 * NZ])
+        seen = (seen[0:width] + seen[width : 2 * width]) + seen[2 * width : 3 * width]
+        for sub in range(8):
+            j = g * 8 + sub
+            mask = iota((GROUPS, NZ), 0) == s_hi[j : j + 1]
+            for c in range(2):
+                at_face = jnp.where(mask, seen[c * GROUPS : (c + 1) * GROUPS, sub * NZ : (sub + 1) * NZ], 0.0)
+                loads[c, j : j + 1, :] = jnp.sum(at_face, axis=0, keepdims=True)
+    sums = [jnp.concatenate([group_sums(q, g) for g in range(SIDE)], axis=0) for q in range(2, 5)]
+    stress = wall_stress(sums[0] - loads[0] * sums[2], sums[1] - loads[1] * sums[2], reynolds)
     for g in range(SIDE):
         eight = slice(g * 8, (g + 1) * 8)
         rsend[g] = jnp.concatenate([stress[0][eight], stress[1][eight]], axis=0)
     for step in range(1, GROUPS):
         stress_copy(step).start()
 
-    load = load_of(stress)
+    load = None
+    for g in range(SIDE):
+        eight = slice(g * 8, (g + 1) * 8)
+        part = group_load((stress[0][eight], stress[1][eight]), g)
+        load = part if load is None else load + part
+    spread = by_cell(load)
     for c in range(2):
         for block in range(CELLS // NZ):
             at = pl.ds(c * SPAN + CY + block * NZ, NZ)
             column = c * GROUPS + block
-            out[pl.ds(c * CELLS + block * NZ, NZ), :] = v1[at, :] - load[:, column : column + 1] * profile
-
+            out[pl.ds(c * CELLS + block * NZ, NZ), :] = v1[at, :] - spread[:, column : column + 1] * profile
+
+    lax.fori_loop(1, CX - 1, second_step, 0)
     for copy in halos2:
         copy.wait_recv()
     for c in range(2):
         v1[pl.ds(c * SPAN + (CX + 1) * CY, CY), :] = hx2[0, pl.ds(c * CY, CY), :]
         v1[pl.ds(c * SPAN, CY), :] = hx2[1, pl.ds(c * CY, CY), :]
-
-    def second_step(x, carry):
-        for c, (v, change) in enumerate(advance(v1, hy2, x)):
-            at = pl.ds(pl.multiple_of(c * CELLS + x * CY, CY), CY)
-            out[at, :] = out[at, :] + change
-        return carry
-
-    lax.fori_loop(0, CX, second_step, 0)
+    second_step(0, 0)
+    second_step(CX - 1, 0)
+    for side, row, sign in ((0, CY - 1, 1.0), (1, 0, -1.0)):
+        factor = factors[2 + side, pl.ds(row, CX, stride=CY), :]
+        factor = factor + (sign * -0.5 * time_step) * v1[pl.ds(SPAN + CY + row, CX, stride=CY), :]
+        for c in range(2):
+            added = hy2[side, pl.ds(c * CX, CX), :] * factor
+            most = CX - 8
+            at = pl.ds(c * CELLS + row, most, stride=CY)
+            out[at, :] = out[at, :] + added[:most]
+            for x in range(most, CX):
+                at = pl.ds(c * CELLS + row + x * CY, 1)
+                out[at, :] = out[at, :] + added[x : x + 1]
 
     for step in range(1, GROUPS):
         stress_copy(step).wait_recv()
     back = jnp.concatenate([four(rsend[0], rrecv, g) for g in range(SIDE)], axis=0)
-    pieces = thirds(back)
+    pieces = jnp.concatenate(thirds(back), axis=0)
+    width = SIDE * 16
     for ch in range(chunks):
         one = slice(ch, ch + 1)
         span = slice(ch * NZ, (ch + 1) * NZ)
         seen = b_face[:, span]
-        spread = mm(pieces[0], seen) + mm(pieces[1], seen) + mm(pieces[2], seen)
+        spread = mm(pieces, seen)
+        spread = (spread[0:width] + spread[width : 2 * width]) + spread[2 * width : 3 * width]
         place = hi_face[one, :]
         row = (place // 8) * 16 + place % 8
         for c in range(2):
@@ -474,7 +517,8 @@
         vm((2 * GROUPS, NZ), i32), pltpu.SMEM((2 * GROUPS, NZ), i32),
         vm((2 * GROUPS, NZ), i32), pltpu.SMEM((2 * GROUPS, NZ), i32),
         vm((4 * CELLS + 8, NZ), f32), vm((4 * CAP + 8, NZ), f32), vm((5 * GROUPS, 8, NZ), f32),
-        vm((NZ, SLOTS), bf16), vm((NZ, SLOTS), bf16), vm((2, 2 * GROUPS, NZ), f32),
+        vm((NZ, SLOTS), bf16), vm((SLOTS, NZ), bf16), vm((6 * GROUPS, 8 * NZ), bf16), vm((2 * GROUPS, NZ), f32),
+        vm((6, CELLS + CY, NZ), f32), vm((2, 2 * GROUPS, NZ), f32),
         vm((2, 3 * CY, NZ), f32), vm((2, 3 * CX, NZ), f32), vm((2, 2 * CY, NZ), f32), vm((2, 2 * CX, NZ), f32),
         vm((2, 3 * CY, NZ), f32), vm((2, 3 * CX, NZ), f32), vm((2, 2 * CY, NZ), f32), vm((2, 2 * CX, NZ), f32),
         vm((SIDE, 16, NZ), f32), vm((GROUPS, 16, NZ), f32),
@@ -494,7 +538,7 @@
         out_specs=(inside, inside),
         scratch_shapes=scratch,
         compiler_params=pltpu.CompilerParams(
-            collective_id=0, has_side_effects=True, vmem_limit_bytes=48 * 1024 * 1024
+            collective_id=0, has_side_effects=True, vmem_limit_bytes=58 * 1024 * 1024
         ),
     )(
         velocity.reshape(2 * CELLS, NZ), metric.reshape(CELLS, NZ), weights,

time: 64.2 us -> 54.7 us (0.85)
  the two profiles are of different devices: /device:TPU:0 before, /device:TPU:48 now
where the time goes in v2:
time: 54.7 us; the launch traced here: 54.6 us
  Pallas kernels  50.2 us (92%)
  local copies, waits for them, and re-layouts  3.69 us (7%)
  between operations  0.65 us (1%)
    pallas_call x1, Pallas kernels, local(): pl.pallas_call(kernel, out_shape=(jax.ShapeDtypeStruct((2 * CELLS, NZ), f...  50.2 us
    unnamed x4, local copies, waits for them, and re-layouts  3.69 us

profile of v2, /device:TPU:48, one launch (start us, length us, event | category | flops | bytes accessed | tf_op | source)
XLA Modules:
  0.0 54.6 jit_solution(6993108004486641762)
XLA Ops:
  0.6 50.2 %shard_map.86 = (f32[4096,128]{1,0:T(8,128)}, f32[2,2048]{1,0:T(2,128)}) custom-call(f32[4096,128]{1,0:T(8,128)} %bitcast.7, f32[2048,128]{1,0:T(8,128)} %bitcast.9, f32[2048,128]{1,0:T(8,128)} %wgt.1, f32[16,128]{1,0:T(8,128)} %bitcast.10, s32[16,128]{1,0:T(8,128)} %bitcast.11, s32[16,128]{1,0:T(8,128)} %bitcast.12, f32[1,128]{1,0:T(1,128)} %bitcast.13), custom_call_target="tpu_custom_call" | custom-call | tf_op jit(solution)/shard_map/pallas_call | solution.py:531
  50.9 0.0 copy-start
  50.9 3.1 %copy.11 = f32[2,64,32,128]{3,2,1,0:T(8,128)} copy(f32[2,64,32,128]{3,2,1,0:T(8,128)} %bitcast.8) | data formatting | bytes 4194304
  54.0 0.0 copy-done
  54.0 0.6 %copy.12 = f32[2,2048]{1,0:T(2,128)} copy(f32[2,2048]{1,0:T(2,128)S(1)} %copy-done) | data formatting | bytes 32768
Async XLA Ops:
  50.9 3.1 %copy-start = (f32[2,2048]{1,0:T(2,128)S(1)}, f32[2,2048]{1,0:T(2,128)}, u32[]{:S(2)}) copy-start(f32[2,2048]{1,0:T(2,128)} %get-tuple-element.9) | copy-start | bytes 49156

commit v3 on v2

--- a/solution.py
+++ b/solution.py
@@ -17,6 +17,7 @@
 CELLS = CX * CY
 SPAN = (CX + 2) * CY
 BLOCK = CAP // 8
+RUN = 4
 
 karman = 0.41
 time_step = 0.2
@@ -71,7 +72,7 @@
     vel, met, wgt, rey_in, tile_in, cell_in, prof_in,
     out, stress_out,
     v0, v1, jac, win, wsend, wrecv, msend, mrecv, lo_face, hi_face, a_face, b_face,
-    meta_cell, meta_rey, cell_v, cell_s, inv_v, inv_s, cols, picked, dots, b_slot, b_rows, a_slot, so_far, factors, loads,
+    meta_cell, meta_rey, cell_v, cell_s, inv_v, inv_s, cols, picked, dots, b_slot, b_rows, a_slot, so_far, factors, slot_hi,
     hx, hy, hx2, hy2, ex, ey, ex2, ey2, rsend, rrecv,
     rey_ref, tile_ref, cell_ref, prof_ref,
     in_sem, smem_sem, ms_sem, mr_sem, ws_sem, wr_sem, hs_sem, hr_sem, rs_sem, rr_sem,
@@ -168,13 +169,16 @@
     slot_rey = (part[4] + part[5]) + part[6]
     to_smem = pltpu.make_async_copy(inv_v, inv_s, smem_sem.at[0])
     to_smem.start()
+    lanes8 = iota((8, NZ), 1) // BLOCK
     for g in range(SIDE):
         eight = slice(g * 8, (g + 1) * 8)
-        msend[g] = jnp.concatenate([slot_cell[eight], slot_rey[eight]], axis=0)
+        beside = pltpu.roll(slot_rey[eight], BLOCK, 1)
+        for k in range(SIDE):
+            msend[g * SIDE + k] = jnp.where(lanes8 == k, slot_cell[eight], beside)
 
     def meta_copy(step):
         return pltpu.make_async_remote_copy(
-            src_ref=msend.at[step // SIDE], dst_ref=mrecv.at[step],
+            src_ref=msend.at[step], dst_ref=mrecv.at[step],
             send_sem=ms_sem.at[step], recv_sem=mr_sem.at[step],
             device_id=(gx, target(step)), device_id_type=MESH,
         )
@@ -188,7 +192,7 @@
 
     def stress_copy(step):
         return pltpu.make_async_remote_copy(
-            src_ref=rsend.at[step // SIDE], dst_ref=rrecv.at[step],
+            src_ref=rsend.at[step], dst_ref=rrecv.at[step],
             send_sem=rs_sem.at[step], recv_sem=rr_sem.at[step],
             device_id=(gx, origin(step)),
             device_id_type=MESH,
@@ -202,26 +206,15 @@
             for k, run in enumerate(runs):
                 target[pl.ds(first + (v * 8 + k) * rows, rows), :] = run
 
-    def pack(step):
-        gather(inv_s, step, win, 1, wsend, step * CAP)
-
-    def pack_send(step, carry):
-        pack(step)
-        weight_copy(step).start()
-        return carry
-
     to_smem.wait()
     loads_in[0].wait()
-    pack(1)
+    gather(inv_s, 1, win, 1, wsend, CAP)
 
     pl.semaphore_wait(barrier, GROUPS + 1)
     for step in range(1, GROUPS):
         meta_copy(step).start()
     weight_copy(1).start()
-    lax.fori_loop(2, 5, pack_send, 0)
-
-    for copy in loads_in[1:]:
-        copy.wait()
+
 
     def edges(buffer, jacobian, x_edge, y_edge):
         for n, at in enumerate((CY, CX * CY)):
@@ -248,34 +241,47 @@
             ))
         return made
 
-    edges(v0, jac, ex, ey)
     halos = halo_copies(ex, ey, hx, hy, 0)
-    for copy in halos:
-        copy.start()
-
-    lax.fori_loop(5, GROUPS, pack_send, 0)
-    pack(0)
+
+    def pack_send(step, carry):
+        gather(inv_s, step, win, 1, wsend, step * CAP)
+        weight_copy(step).start()
+
+        @pl.when(step == 4)
+        def _():
+            for copy in loads_in[1:]:
+                copy.wait()
+            edges(v0, jac, ex, ey)
+            for copy in halos:
+                copy.start()
+
+        return carry
+
+    lax.fori_loop(2, GROUPS, pack_send, 0)
+    gather(inv_s, 0, win, 1, wrecv, 0)
 
     for step in range(1, GROUPS):
         meta_copy(step).wait_recv()
-    lanes16 = iota((16, NZ), 1) // BLOCK
 
     def four(first, received, g):
-        rows = first if g == 0 else received[g * SIDE]
+        tiles = [first if g + k == 0 else received[g * SIDE + k] for k in range(SIDE)]
+        rows, others = tiles[0], tiles[SIDE - 1]
         for k in range(1, SIDE):
-            rows = jnp.where(lanes16 == k, received[g * SIDE + k], rows)
-        return rows
+            rows = jnp.where(lanes8 == k, tiles[k], rows)
+            others = jnp.where(lanes8 == k, tiles[k - 1], others)
+        return rows, pltpu.roll(others, NZ - BLOCK, 1)
 
     for g in range(SIDE):
-        rows = four(msend[0], mrecv, g)
-        meta_cell[g * 8 : (g + 1) * 8, :] = rows[0:8]
-        meta_rey[g * 8 : (g + 1) * 8, :] = rows[8:16]
+        rows, others = four(msend[0], mrecv, g)
+        meta_cell[g * 8 : (g + 1) * 8, :] = rows
+        meta_rey[g * 8 : (g + 1) * 8, :] = others
     slot_of = meta_cell[...].astype(i32)
     cell_v[...] = jnp.clip(slot_of, 0, CELLS - 1) * 4
     cells_smem = pltpu.make_async_copy(cell_v, cell_s, smem_sem.at[1])
     cells_smem.start()
     used = slot_of >= 0
     s_hi = jnp.where(used, slot_of // NZ, -1)
+    slot_hi[...] = s_hi
     s_lo = jnp.where(used, slot_of % NZ, -1)
     for j in range(2 * GROUPS):
         seen = (iota((NZ, NZ), 0) == s_lo[j : j + 1]).astype(f32)
@@ -288,7 +294,6 @@
     row_y = iota((CY, NZ), 0)
     lane = iota((CY, NZ), 1)
     at_first, at_last = row_y == 0, row_y == CY - 1
-    top, bottom = lane == NZ - 1, lane == 0
 
     for c in range(2):
         v0[pl.ds(c * SPAN + (CX + 1) * CY, CY), :] = hx[0, pl.ds(c * CY, CY), :]
@@ -307,9 +312,9 @@
         last_y = jnp.where(at_first, halo[1, pl.ds(row + x, 1), :], last_y)
         return centre, next_x, last_x, next_y, last_y
 
-    def column_sum(v):
-        above = jnp.where(top, 0.0, pltpu.roll(v, NZ - 1, 1))
-        below = jnp.where(bottom, 0.0, pltpu.roll(v, 1, 1))
+    def column_sum(v, level):
+        above = jnp.where(level == NZ - 1, 0.0, pltpu.roll(v, NZ - 1, 1))
+        below = jnp.where(level == 0, 0.0, pltpu.roll(v, 1, 1))
         return above + below
 
     def first_step(x, carry):
@@ -328,43 +333,50 @@
         k_e, k_w, k_n, k_s = k_e + along, k_w - along, k_n + across, k_s - across
         for c in range(2):
             v, e, w, n, s = stars[c]
-            new = v + ((k_e * e + k_w * w) + (k_n * n + k_s * s) + (k_v * column_sum(v) - k_c * v))
+            new = v + ((k_e * e + k_w * w) + (k_n * n + k_s * s) + (k_v * column_sum(v, lane) - k_c * v))
             v1[pl.ds(pl.multiple_of(c * SPAN + (x + 1) * CY, CY), CY), :] = new
             cols[pl.ds(x * (4 * CY) + c, CY, stride=4), :] = v
             cols[pl.ds(x * (4 * CY) + 2 + c, CY, stride=4), :] = new
         return carry
 
-    def second_step(x, carry):
-        at = pl.ds(pl.multiple_of(x * CY, CY), CY)
+    tall = RUN * CY
+    y_tall, lane_tall = iota((tall, NZ), 0) % CY, iota((tall, NZ), 1)
+
+    def second_step(run, carry):
+        x = run * RUN
+        at = pl.ds(pl.multiple_of(x * CY, tall), tall)
         k_e, k_w, k_n, k_s, k_v, k_c = [factors[n, at, :] for n in range(6)]
         here = [pl.multiple_of(c * SPAN + (x + 1) * CY, CY) for c in range(2)]
-        centre = [v1[pl.ds(here[c], CY), :] for c in range(2)]
+        centre = [v1[pl.ds(here[c], tall), :] for c in range(2)]
         along = (-0.5 * time_step) * centre[0]
         across = (-0.5 * time_step) * centre[1]
         k_e, k_w = k_e + along, k_w - along
-        k_n = jnp.where(at_last, 0.0, k_n + across)
-        k_s = jnp.where(at_first, 0.0, k_s - across)
+        k_n = jnp.where(y_tall == CY - 1, 0.0, k_n + across)
+        k_s = jnp.where(y_tall == 0, 0.0, k_s - across)
         for c in range(2):
             v = centre[c]
-            e = v1[pl.ds(pl.multiple_of(here[c] + CY, CY), CY), :]
-            w = v1[pl.ds(pl.multiple_of(here[c] - CY, CY), CY), :]
-            n = v1[pl.ds(here[c] + 1, CY), :]
-            s = v1[pl.ds(here[c] - 1, CY), :]
-            change = (k_e * e + k_w * w) + (k_n * n + k_s * s) + (k_v * column_sum(v) - k_c * v)
-            at = pl.ds(pl.multiple_of(c * CELLS + x * CY, CY), CY)
+            e = v1[pl.ds(pl.multiple_of(here[c] + CY, CY), tall), :]
+            w = v1[pl.ds(pl.multiple_of(here[c] - CY, CY), tall), :]
+            n = v1[pl.ds(here[c] + 1, tall), :]
+            s = v1[pl.ds(here[c] - 1, tall), :]
+            change = (k_e * e + k_w * w) + (k_n * n + k_s * s) + (k_v * column_sum(v, lane_tall) - k_c * v)
+            at = pl.ds(pl.multiple_of(c * CELLS + x * CY, tall), tall)
             out[at, :] = out[at, :] + change
         return carry
 
-    lax.fori_loop(0, CX, first_step, 0)
+    def first_pair(pair, carry):
+        return first_step(2 * pair + 1, first_step(2 * pair, carry))
+
+    lax.fori_loop(0, CX // 2, first_pair, 0)
 
     cells_smem.wait()
     profile = prof_ref[...]
 
     lane8 = iota((8, NZ), 1) % BLOCK
 
-    def chunk(step, source):
+    def chunk(step):
         gather(cell_s, step, cols, 4, picked, 0)
-        weights = source[pl.ds(pl.multiple_of(step * CAP, CAP), CAP), :]
+        weights = wrecv[pl.ds(pl.multiple_of(step * CAP, CAP), CAP), :]
         for q in range(5):
             if q < 4:
                 product = picked[pl.ds(q, CAP, stride=4), :] * weights
@@ -377,11 +389,12 @@
             dots[pl.ds(q * GROUPS + step, 1)] = rows.reshape(1, 8, NZ)
 
     def arrived(step, carry):
-        weight_copy(step).wait_recv()
-        chunk(step, wrecv)
+        @pl.when(step > 0)
+        def _():
+            weight_copy(step).wait_recv()
+
+        chunk(step)
         return carry
-
-    lanes8 = iota((8, NZ), 1) // BLOCK
 
     def group_sums(q, g):
         rows = dots[q * GROUPS + g * SIDE]
@@ -389,32 +402,32 @@
             rows = jnp.where(lanes8 == k, dots[q * GROUPS + g * SIDE + k], rows)
         return rows
 
+    def eight_rows(ref, g):
+        return ref[pl.ds(g * 8 if isinstance(g, int) else pl.multiple_of(g * 8, 8), 8), :]
+
     def group_load(stress, g):
-        eight = slice(g * 8, (g + 1) * 8)
-        pieces = [[p.astype(f32) for p in thirds(jnp.where(used[eight], s, 0.0))] for s in stress]
+        high = eight_rows(slot_hi, g)
+        pieces = [[p.astype(f32) for p in thirds(jnp.where(high >= 0, s, 0.0))] for s in stress]
         for sub in range(8):
             one = slice(sub, sub + 1)
-            mask = iota((GROUPS, NZ), 0) == s_hi[g * 8 + sub : g * 8 + sub + 1]
+            mask = iota((GROUPS, NZ), 0) == high[one]
             parts = [jnp.where(mask, pieces[c][k][one], 0.0) for k in range(3) for c in range(2)]
             a_slot[:, sub * NZ : (sub + 1) * NZ] = jnp.concatenate(parts, axis=0).astype(bf16)
-        total = mm(a_slot[...], b_rows[g * 8 * NZ : (g + 1) * 8 * NZ, :])
+        total = mm(a_slot[...], b_rows[pl.ds((g * 8 * NZ if isinstance(g, int) else pl.multiple_of(g * 8 * NZ, 8 * NZ)), 8 * NZ), :])
         width = 2 * GROUPS
-        return (total[0:width] + total[width : 2 * width]) + total[2 * width : 3 * width]
+        so_far[...] = so_far[...] + ((total[0:width] + total[width : 2 * width]) + total[2 * width : 3 * width])
 
     def by_cell(load):
         return jnp.transpose(jnp.concatenate([load, jnp.zeros((NZ - 2 * GROUPS, NZ), f32)], axis=0))
 
-    reynolds = meta_rey[...]
-    load = None
-    for g in range(SIDE):
-        if g == 0:
-            chunk(0, wsend)
-        lax.fori_loop(max(1, g * SIDE), (g + 1) * SIDE, arrived, 0)
-        part = group_load(wall_stress(group_sums(0, g), group_sums(1, g), reynolds[g * 8 : (g + 1) * 8]), g)
-        if g < SIDE - 1:
-            so_far[...] = part if g == 0 else so_far[...] + part
-        else:
-            load = so_far[...] + part
+    def group(g, carry):
+        lax.fori_loop(g * SIDE, (g + 1) * SIDE, arrived, 0)
+        group_load(wall_stress(group_sums(0, g), group_sums(1, g), eight_rows(meta_rey, g)), g)
+        return carry
+
+    so_far[...] = jnp.zeros((2 * GROUPS, NZ), f32)
+    lax.fori_loop(0, SIDE, group, 0)
+    load = so_far[...]
 
     spread = by_cell(load)
     for c in range(2):
@@ -430,28 +443,35 @@
 
     pieces = jnp.concatenate(thirds(load), axis=0)
     width = 2 * GROUPS
-    for g in range(SIDE):
-        seen = mm(pieces, b_slot[:, g * 8 * NZ : (g + 1) * 8 * NZ])
+    so_far[...] = jnp.zeros((2 * GROUPS, NZ), f32)
+
+    def second_group(g, carry):
+        high = eight_rows(slot_hi, g)
+        seen = mm(pieces, b_slot[:, pl.ds((g * 8 * NZ if isinstance(g, int) else pl.multiple_of(g * 8 * NZ, 8 * NZ)), 8 * NZ)])
         seen = (seen[0:width] + seen[width : 2 * width]) + seen[2 * width : 3 * width]
+        met_load = [[], []]
         for sub in range(8):
-            j = g * 8 + sub
-            mask = iota((GROUPS, NZ), 0) == s_hi[j : j + 1]
+            mask = iota((GROUPS, NZ), 0) == high[sub : sub + 1]
             for c in range(2):
                 at_face = jnp.where(mask, seen[c * GROUPS : (c + 1) * GROUPS, sub * NZ : (sub + 1) * NZ], 0.0)
-                loads[c, j : j + 1, :] = jnp.sum(at_face, axis=0, keepdims=True)
-    sums = [jnp.concatenate([group_sums(q, g) for g in range(SIDE)], axis=0) for q in range(2, 5)]
-    stress = wall_stress(sums[0] - loads[0] * sums[2], sums[1] - loads[1] * sums[2], reynolds)
-    for g in range(SIDE):
-        eight = slice(g * 8, (g + 1) * 8)
-        rsend[g] = jnp.concatenate([stress[0][eight], stress[1][eight]], axis=0)
+                met_load[c].append(jnp.sum(at_face, axis=0, keepdims=True))
+        met_load = [jnp.concatenate(rows, axis=0) for rows in met_load]
+        shape = group_sums(4, g)
+        stress = wall_stress(
+            group_sums(2, g) - met_load[0] * shape, group_sums(3, g) - met_load[1] * shape, eight_rows(meta_rey, g)
+        )
+        beside = pltpu.roll(stress[1], BLOCK, 1)
+        for k in range(SIDE):
+            rsend[g * SIDE + k] = jnp.where(lanes8 == k, stress[0], beside)
+        return stress
+
+    stresses = [second_group(g, 0) for g in range(SIDE)]
     for step in range(1, GROUPS):
         stress_copy(step).start()
-
-    load = None
     for g in range(SIDE):
-        eight = slice(g * 8, (g + 1) * 8)
-        part = group_load((stress[0][eight], stress[1][eight]), g)
-        load = part if load is None else load + part
+        group_load(stresses[g], g)
+
+    load = so_far[...]
     spread = by_cell(load)
     for c in range(2):
         for block in range(CELLS // NZ):
@@ -459,14 +479,13 @@
             column = c * GROUPS + block
             out[pl.ds(c * CELLS + block * NZ, NZ), :] = v1[at, :] - spread[:, column : column + 1] * profile
 
-    lax.fori_loop(1, CX - 1, second_step, 0)
+    lax.fori_loop(1, CX // RUN - 1, second_step, 0)
     for copy in halos2:
         copy.wait_recv()
     for c in range(2):
         v1[pl.ds(c * SPAN + (CX + 1) * CY, CY), :] = hx2[0, pl.ds(c * CY, CY), :]
         v1[pl.ds(c * SPAN, CY), :] = hx2[1, pl.ds(c * CY, CY), :]
-    second_step(0, 0)
-    second_step(CX - 1, 0)
+    lax.fori_loop(0, 2, lambda n, carry: second_step(n * (CX // RUN - 1), carry), 0)
     for side, row, sign in ((0, CY - 1, 1.0), (1, 0, -1.0)):
         factor = factors[2 + side, pl.ds(row, CX, stride=CY), :]
         factor = factor + (sign * -0.5 * time_step) * v1[pl.ds(SPAN + CY + row, CX, stride=CY), :]
@@ -481,7 +500,7 @@
 
     for step in range(1, GROUPS):
         stress_copy(step).wait_recv()
-    back = jnp.concatenate([four(rsend[0], rrecv, g) for g in range(SIDE)], axis=0)
+    back = jnp.concatenate([rows for g in range(SIDE) for rows in four(rsend[0], rrecv, g)], axis=0)
     pieces = jnp.concatenate(thirds(back), axis=0)
     width = SIDE * 16
     for ch in range(chunks):
@@ -511,17 +530,17 @@
     scratch = [
         vm((2 * SPAN, NZ), f32), vm((2 * SPAN, NZ), f32), vm((SPAN, NZ), f32), vm((FACES, NZ), f32),
         vm((SLOTS, NZ), f32), vm((SLOTS, NZ), f32),
-        vm((SIDE, 16, NZ), f32), vm((GROUPS, 16, NZ), f32),
+        vm((GROUPS, 8, NZ), f32), vm((GROUPS, 8, NZ), f32),
         vm(small, i32), vm(small, i32), vm((14 * GROUPS, FACES), bf16), vm((NZ, FACES), bf16),
         vm((2 * GROUPS, NZ), f32), vm((2 * GROUPS, NZ), f32),
         vm((2 * GROUPS, NZ), i32), pltpu.SMEM((2 * GROUPS, NZ), i32),
         vm((2 * GROUPS, NZ), i32), pltpu.SMEM((2 * GROUPS, NZ), i32),
         vm((4 * CELLS + 8, NZ), f32), vm((4 * CAP + 8, NZ), f32), vm((5 * GROUPS, 8, NZ), f32),
         vm((NZ, SLOTS), bf16), vm((SLOTS, NZ), bf16), vm((6 * GROUPS, 8 * NZ), bf16), vm((2 * GROUPS, NZ), f32),
-        vm((6, CELLS + CY, NZ), f32), vm((2, 2 * GROUPS, NZ), f32),
+        vm((6, CELLS + CY, NZ), f32), vm((2 * GROUPS, NZ), i32),
         vm((2, 3 * CY, NZ), f32), vm((2, 3 * CX, NZ), f32), vm((2, 2 * CY, NZ), f32), vm((2, 2 * CX, NZ), f32),
         vm((2, 3 * CY, NZ), f32), vm((2, 3 * CX, NZ), f32), vm((2, 2 * CY, NZ), f32), vm((2, 2 * CX, NZ), f32),
-        vm((SIDE, 16, NZ), f32), vm((GROUPS, 16, NZ), f32),
+        vm((GROUPS, 8, NZ), f32), vm((GROUPS, 8, NZ), f32),
         vm(small, f32), vm(small, i32), vm(small, i32), vm((1, NZ), f32),
         dma((8,)), dma((2,)), dma((GROUPS,)), dma((GROUPS,)), dma((GROUPS,)), dma((GROUPS,)),
         dma((8,)), dma((8,)), dma((GROUPS,)), dma((GROUPS,)),
@@ -538,12 +557,12 @@
         out_specs=(inside, inside),
         scratch_shapes=scratch,
         compiler_params=pltpu.CompilerParams(
-            collective_id=0, has_side_effects=True, vmem_limit_bytes=58 * 1024 * 1024
+            collective_id=0, has_side_effects=True, vmem_limit_bytes=48 * 1024 * 1024
         ),
-    )(
+    )(*[pltpu.with_memory_space_constraint(array, pltpu.HBM) for array in (
         velocity.reshape(2 * CELLS, NZ), metric.reshape(CELLS, NZ), weights,
         reynolds.reshape(small), face_tile.reshape(small), face_cell.reshape(small), profile.reshape(1, NZ),
-    )
+    )])
     return out.reshape(2, CX, CY, NZ), stress
 
 

time: 54.7 us -> 49.8 us (0.910)
  the two profiles are of different devices: /device:TPU:48 before, /device:TPU:0 now
where the time goes in v3:
time: 49.8 us; the launch traced here: 49.7 us
  Pallas kernels  47.1 us (95%)
  local copies, waits for them, and re-layouts  1.93 us (4%)
  between operations  0.64 us (1%)
    pallas_call x1, Pallas kernels, local(): pl.pallas_call(kernel, out_shape=(jax.ShapeDtypeStruct((2 * CELLS, NZ), f...  47.1 us
    unnamed x2, local copies, waits for them, and re-layouts  1.93 us

profile of v3, /device:TPU:0, one launch (start us, length us, event | category | flops | bytes accessed | tf_op | source)
XLA Modules:
  0.0 49.7 jit_solution(368460213373503738)
XLA Ops:
  0.6 47.1 %shard_map.86 = (f32[4096,128]{1,0:T(8,128)S(1)}, f32[2,2048]{1,0:T(2,128)S(1)}) custom-call(f32[4096,128]{1,0:T(8,128)} %bitcast.8, f32[2048,128]{1,0:T(8,128)} %bitcast.9, f32[2048,128]{1,0:T(8,128)} %wgt.1, f32[16,128]{1,0:T(8,128)} %bitcast.10, s32[16,128]{1,0:T(8,128)} %bitcast.11, s32[16,128]{1,0:T(8,128)} %bitcast.12, f32[1,128]{1,0:T(1,128)} %bitcast.13), custom_call_target="tpu_custom_call" | custom-call | tf_op jit(solution)/shard_map/pallas_call | solution.py:550
  47.8 1.3 %copy.11 = f32[2,64,32,128]{3,2,1,0:T(8,128)} copy(f32[2,64,32,128]{3,2,1,0:T(8,128)S(1)} %bitcast.7) | data formatting | bytes 4194304
  49.1 0.6 %copy.12 = f32[2,2048]{1,0:T(2,128)} copy(f32[2,2048]{1,0:T(2,128)S(1)} %get-tuple-element.9) | data formatting | bytes 32768

commit v4 on v3

--- a/solution.py
+++ b/solution.py
@@ -18,6 +18,7 @@
 SPAN = (CX + 2) * CY
 BLOCK = CAP // 8
 RUN = 4
+PIECES = 4
 
 karman = 0.41
 time_step = 0.2
@@ -30,7 +31,7 @@
 
 NT = (((1,), (1,)), ((), ()))
 
-ORDER = (0, 4, 12, 1, 3, 8, 2, 5, 15, 7, 13, 10, 6, 14, 9, 11)
+ORDER = (0, 10, 4, 12, 1, 3, 6, 14, 9, 11, 8, 2, 5, 15, 7, 13)
 
 
 def iota(shape, dim):
@@ -211,8 +212,6 @@
     gather(inv_s, 1, win, 1, wsend, CAP)
 
     pl.semaphore_wait(barrier, GROUPS + 1)
-    for step in range(1, GROUPS):
-        meta_copy(step).start()
     weight_copy(1).start()
 
 
@@ -246,6 +245,11 @@
     def pack_send(step, carry):
         gather(inv_s, step, win, 1, wsend, step * CAP)
         weight_copy(step).start()
+
+        @pl.when(step == 3)
+        def _():
+            for other in range(1, GROUPS):
+                meta_copy(other).start()
 
         @pl.when(step == 4)
         def _():
@@ -412,8 +416,8 @@
             one = slice(sub, sub + 1)
             mask = iota((GROUPS, NZ), 0) == high[one]
             parts = [jnp.where(mask, pieces[c][k][one], 0.0) for k in range(3) for c in range(2)]
-            a_slot[:, sub * NZ : (sub + 1) * NZ] = jnp.concatenate(parts, axis=0).astype(bf16)
-        total = mm(a_slot[...], b_rows[pl.ds((g * 8 * NZ if isinstance(g, int) else pl.multiple_of(g * 8 * NZ, 8 * NZ)), 8 * NZ), :])
+            a_slot[g, :, sub * NZ : (sub + 1) * NZ] = jnp.concatenate(parts, axis=0).astype(bf16)
+        total = mm(a_slot[g], b_rows[pl.ds((g * 8 * NZ if isinstance(g, int) else pl.multiple_of(g * 8 * NZ, 8 * NZ)), 8 * NZ), :])
         width = 2 * GROUPS
         so_far[...] = so_far[...] + ((total[0:width] + total[width : 2 * width]) + total[2 * width : 3 * width])
 
@@ -480,6 +484,11 @@
             out[pl.ds(c * CELLS + block * NZ, NZ), :] = v1[at, :] - spread[:, column : column + 1] * profile
 
     lax.fori_loop(1, CX // RUN - 1, second_step, 0)
+    for copy in halos:
+        copy.wait_send()
+    for step in range(1, GROUPS):
+        meta_copy(step).wait_send()
+        weight_copy(step).wait_send()
     for copy in halos2:
         copy.wait_recv()
     for c in range(2):
@@ -515,12 +524,22 @@
             mask = iota((SIDE * 16, NZ), 0) == row + c * 8
             stress_out[c : c + 1, span] = jnp.sum(jnp.where(mask, spread, 0.0), axis=0, keepdims=True)
 
-    for copy in halos + halos2:
+    for copy in halos2:
         copy.wait_send()
     for step in range(1, GROUPS):
-        meta_copy(step).wait_send()
-        weight_copy(step).wait_send()
         stress_copy(step).wait_send()
+
+
+def write_out(velocity, stress, velocity_out, stress_out, sem):
+    rows = 2 * CELLS // PIECES
+    copies = [pltpu.make_async_copy(stress, stress_out, sem.at[PIECES])]
+    for n in range(PIECES):
+        part = pl.ds(n * rows, rows)
+        copies.append(pltpu.make_async_copy(velocity.at[part], velocity_out.at[part], sem.at[n]))
+    for copy in copies:
+        copy.start()
+    for copy in copies:
+        copy.wait()
 
 
 def local(velocity, metric, weights, reynolds, face_tile, face_cell, profile):
@@ -536,7 +555,7 @@
         vm((2 * GROUPS, NZ), i32), pltpu.SMEM((2 * GROUPS, NZ), i32),
         vm((2 * GROUPS, NZ), i32), pltpu.SMEM((2 * GROUPS, NZ), i32),
         vm((4 * CELLS + 8, NZ), f32), vm((4 * CAP + 8, NZ), f32), vm((5 * GROUPS, 8, NZ), f32),
-        vm((NZ, SLOTS), bf16), vm((SLOTS, NZ), bf16), vm((6 * GROUPS, 8 * NZ), bf16), vm((2 * GROUPS, NZ), f32),
+        vm((NZ, SLOTS), bf16), vm((SLOTS, NZ), bf16), vm((SIDE, 6 * GROUPS, 8 * NZ), bf16), vm((2 * GROUPS, NZ), f32),
         vm((6, CELLS + CY, NZ), f32), vm((2 * GROUPS, NZ), i32),
         vm((2, 3 * CY, NZ), f32), vm((2, 3 * CX, NZ), f32), vm((2, 2 * CY, NZ), f32), vm((2, 2 * CX, NZ), f32),
         vm((2, 3 * CY, NZ), f32), vm((2, 3 * CX, NZ), f32), vm((2, 2 * CY, NZ), f32), vm((2, 2 * CX, NZ), f32),
@@ -550,8 +569,8 @@
     out, stress = pl.pallas_call(
         kernel,
         out_shape=(
-            jax.ShapeDtypeStruct((2 * CELLS, NZ), f32),
-            jax.ShapeDtypeStruct((2, FACES), f32),
+            pltpu.VMEM((2 * CELLS, NZ), f32),
+            pltpu.VMEM((2, FACES), f32),
         ),
         in_specs=[whole] * 7,
         out_specs=(inside, inside),
@@ -563,6 +582,17 @@
         velocity.reshape(2 * CELLS, NZ), metric.reshape(CELLS, NZ), weights,
         reynolds.reshape(small), face_tile.reshape(small), face_cell.reshape(small), profile.reshape(1, NZ),
     )])
+    out, stress = pl.pallas_call(
+        write_out,
+        out_shape=(
+            jax.ShapeDtypeStruct((2 * CELLS, NZ), f32),
+            jax.ShapeDtypeStruct((2, FACES), f32),
+        ),
+        in_specs=[inside, inside],
+        out_specs=(whole, whole),
+        scratch_shapes=[dma((PIECES + 1,))],
+        compiler_params=pltpu.CompilerParams(vmem_limit_bytes=4 * 1024 * 1024),
+    )(*[pltpu.with_memory_space_constraint(array, pltpu.VMEM) for array in (out, stress)])
     return out.reshape(2, CX, CY, NZ), stress
 
 

time: 49.8 us -> 47.6 us (0.956)
  the two profiles are of different devices: /device:TPU:0 before, /device:TPU:1 now
where the time goes in v4:
time: 47.6 us; the launch traced here: 47.5 us
  Pallas kernels  46.8 us (98%)
  between operations  0.64 us (1%)
    pallas_call x1, Pallas kernels, local(): pl.pallas_call(kernel, out_shape=(pltpu.VMEM((2 * CELLS, NZ), f32), pltpu...  45.5 us
    pallas_call x1, Pallas kernels, local(): pl.pallas_call(write_out, out_shape=(jax.ShapeDtypeStruct((2 * CELLS, NZ)...  1.36 us

profile of v4, /device:TPU:1, one launch (start us, length us, event | category | flops | bytes accessed | tf_op | source)
XLA Modules:
  0.0 47.5 jit_solution(16955848174054607929)
XLA Ops:
  0.6 45.5 %shard_map.86 = (f32[4096,128]{1,0:T(8,128)S(1)}, f32[2,2048]{1,0:T(2,128)S(1)}) custom-call(f32[4096,128]{1,0:T(8,128)} %bitcast.7, f32[2048,128]{1,0:T(8,128)} %bitcast.8, f32[2048,128]{1,0:T(8,128)} %wgt.1, f32[16,128]{1,0:T(8,128)} %bitcast.9, s32[16,128]{1,0:T(8,128)} %bitcast.10, s32[16,128]{1,0:T(8,128)} %bitcast.11, f32[1,128]{1,0:T(1,128)} %bitcast.12), custom_call_target="tpu_custom_call" | custom-call | tf_op jit(solution)/shard_map/pallas_call | solution.py:569
  46.1 1.4 %shard_map.87 = (f32[4096,128]{1,0:T(8,128)}, f32[2,2048]{1,0:T(2,128)}) custom-call(f32[4096,128]{1,0:T(8,128)S(1)} %get-tuple-element.6.velocity, f32[2,2048]{1,0:T(2,128)S(1)} %get-tuple-element.7.stress), custom_call_target="tpu_custom_call" | custom-call | tf_op jit(solution)/shard_map/pallas_call | solution.py:585

commit v5 on v4

--- a/solution.py
+++ b/solution.py
@@ -251,7 +251,7 @@
             for other in range(1, GROUPS):
                 meta_copy(other).start()
 
-        @pl.when(step == 4)
+        @pl.when(step == 2)
         def _():
             for copy in loads_in[1:]:
                 copy.wait()

time: 47.6 us -> 47.2 us (level)
  the two profiles are of different devices: /device:TPU:1 before, /device:TPU:0 now
where the time goes in v5:
time: 47.2 us; the launch traced here: 46.5 us
  Pallas kernels  45.9 us (97%)
  between operations  0.64 us (1%)
    pallas_call x1, Pallas kernels, local(): pl.pallas_call(kernel, out_shape=(pltpu.VMEM((2 * CELLS, NZ), f32), pltpu...  44.5 us
    pallas_call x1, Pallas kernels, local(): pl.pallas_call(write_out, out_shape=(jax.ShapeDtypeStruct((2 * CELLS, NZ)...  1.36 us

profile of v5, /device:TPU:0, one launch (start us, length us, event | category | flops | bytes accessed | tf_op | source)
XLA Modules:
  0.0 46.5 jit_solution(6706402085096580894)
XLA Ops:
  0.6 44.5 %shard_map.86 = (f32[4096,128]{1,0:T(8,128)S(1)}, f32[2,2048]{1,0:T(2,128)S(1)}) custom-call(f32[4096,128]{1,0:T(8,128)} %bitcast.7, f32[2048,128]{1,0:T(8,128)} %bitcast.8, f32[2048,128]{1,0:T(8,128)} %wgt.1, f32[16,128]{1,0:T(8,128)} %bitcast.9, s32[16,128]{1,0:T(8,128)} %bitcast.10, s32[16,128]{1,0:T(8,128)} %bitcast.11, f32[1,128]{1,0:T(1,128)} %bitcast.12), custom_call_target="tpu_custom_call" | custom-call | tf_op jit(solution)/shard_map/pallas_call | solution.py:569
  45.1 1.4 %shard_map.87 = (f32[4096,128]{1,0:T(8,128)}, f32[2,2048]{1,0:T(2,128)}) custom-call(f32[4096,128]{1,0:T(8,128)S(1)} %get-tuple-element.6.velocity, f32[2,2048]{1,0:T(2,128)S(1)} %get-tuple-element.7.stress), custom_call_target="tpu_custom_call" | custom-call | tf_op jit(solution)/shard_map/pallas_call | solution.py:585
